TPU v7x, 128 devices: a whole 4x4x4 slice. The times are simulated.
128 devices in a mesh: dp: 32 (over x, z, y_hi), tensor: 4 (over y_lo, core).
Axes of the slice: x: 4, y: 4 (y_hi: 2, y_lo: 2; y = y_hi * 2 + y_lo), z: 4, core: 2. Of those that a mesh axis runs over, the one named last changes fastest.
Arguments:
- hidden_in: bfloat16 [32768, 1024], P(('dp', 'tensor')), may hold values from -6 to 6
- out_grad: bfloat16 [32768, 1024], P(('dp', 'tensor')), may hold values from -6 to 6
- attn_gain: bfloat16 [1024], P('dp'), may hold values from 0.5 to 1.5
- query_weight: bfloat16 [1024, 1024], P('dp', 'tensor'), may hold values from -0.1875 to 0.1875
- key_weight: bfloat16 [1024, 512], P('dp', 'tensor'), may hold values from -0.1875 to 0.1875
- value_weight: bfloat16 [1024, 512], P('dp', 'tensor'), may hold values from -0.1875 to 0.1875
- output_weight: bfloat16 [1024, 1024], P('dp', 'tensor'), may hold values from -1.5 to 1.5
- moe_gain: bfloat16 [1024], P('dp'), may hold values from 0.5 to 1.5
- router_weight: bfloat16 [1024, 32], P('dp'), may hold values from -0.09375 to 0.09375
- expert_gate: bfloat16 [32, 1024, 512], P(None, 'dp', 'tensor'), may hold values from -0.1875 to 0.1875
- expert_up: bfloat16 [32, 1024, 512], P(None, 'dp', 'tensor'), may hold values from -0.1875 to 0.1875
- expert_down: bfloat16 [32, 1024, 512], P(None, 'dp', 'tensor'), may hold values from -1 to 1
- expert_ids: int32 [32768, 8], P(('dp', 'tensor')), may hold values from 0 to 31, all different within a row; in each aligned block of 1024 rows (0 to 1023, 1024 to 2047, ...) at most 320 rows name the same one
- segment_ids: int32 [32768], P(('dp', 'tensor')), may hold values from 0 to 3, as said below
Outputs:
- block_out: bfloat16 [32768, 1024], P(('dp', 'tensor'))
- hidden_grad: float32 [32768, 1024], P(('dp', 'tensor'))
- attn_gain_grad: float32 [1024], P('dp')
- query_grad: float32 [1024, 1024], P('dp', 'tensor')
- key_grad: float32 [1024, 512], P('dp', 'tensor')
- value_grad: float32 [1024, 512], P('dp', 'tensor')
- output_grad: float32 [1024, 1024], P('dp', 'tensor')
- moe_gain_grad: float32 [1024], P('dp')
- router_grad: float32 [1024, 32], P('dp')
- expert_gate_grad: float32 [32, 1024, 512], P(None, 'dp', 'tensor')
- expert_up_grad: float32 [32, 1024, 512], P(None, 'dp', 'tensor')
- expert_down_grad: float32 [32, 1024, 512], P(None, 'dp', 'tensor')
Inputs may be any that keep to these rules, and one draw needn't show every extreme that they name: `expert_ids`: each row names 8 different experts. Within the rows of one sequence no expert is named by more than 320 rows, and in some sequence some expert is named by exactly 320. `segment_ids`: each sequence of 1024 tokens holds four documents numbered 0, 1, 2, 3, never falling, each of one token or more; document 1 begins in the first quarter of its sequence and ends in the last quarter.
All inputs are finite; a program needn't handle non-finite values.
Results may differ from a plain program's by a relative error of at most 0.028.
Values may be sent and summed in bfloat16 or wider, within the bound.
A program may use at most 320 MiB of HBM per device.

v0:
```python
import math

import jax
import jax.numpy as jnp
from jax import lax
from jax.sharding import PartitionSpec as P

D = 1024
HD = 64
E = 32
TOPK = 8


epsilon = 1e-06
masked_score = -1e30
contract_rows = (((0,), (0,)), ((), ()))
contract_last = (((1,), (1,)), ((), ()))


def from_everyone(value, axis):
    count = lax.axis_size(axis)
    return lax.all_to_all(
        jnp.broadcast_to(value[None], (count, *value.shape)), axis, 0, 0, tiled=True
    )


def laid_out(tiles, dim):
    tiles = jnp.moveaxis(tiles, 0, dim)
    dims = tiles.shape
    return tiles.reshape(*dims[:dim], dims[dim] * dims[dim + 1], *dims[dim + 2 :])


def gather_directly(value, axis, dim):
    tiles = from_everyone(value, axis)
    return laid_out(tiles, dim)


def split_up(value, dim, count):
    before, after = (value.shape[:dim], value.shape[dim + 1 :])
    return jnp.moveaxis(value.reshape(*before, count, -1, *after), dim, 0)


def sent_and_summed(value, axis, dim):
    tiles = split_up(value, dim, lax.axis_size(axis))
    arrived = lax.all_to_all(tiles, axis, split_axis=0, concat_axis=0, tiled=True)
    return arrived.sum(axis=0)


def turned_gather(arrays, axis, dims):
    turned = [jnp.moveaxis(a, dim, 0) for a, dim in zip(arrays, dims)]
    widths = [t[0].size for t in turned]
    both = jnp.concatenate([t.reshape(-1, w) for t, w in zip(turned, widths)], axis=1)
    whole = lax.all_gather(both, axis, axis=0, tiled=True)
    tiles = jnp.split(whole, [sum(widths[:k]) for k in range(1, len(widths))], axis=1)
    return tuple(
        (
            jnp.moveaxis(b.reshape(-1, *t.shape[1:]), 0, dim)
            for b, t, dim in zip(tiles, turned, dims)
        )
    )


def in_one_piece(arrays, axis, dim, along):
    widths = [a.shape[along] for a in arrays]
    both = jnp.concatenate(arrays, axis=along)
    whole = lax.all_gather(both, axis, axis=dim, tiled=True)
    return tuple(jnp.split(whole, [sum(widths[:k]) for k in range(1, len(widths))], axis=along))


def in_one_piece_2(arrays, axis, dim, along):
    columns = [a.reshape(*a.shape[:along], -1) for a in arrays]
    both = jnp.concatenate(columns, axis=along)
    whole, at, finished = (lax.all_gather(both, axis, axis=dim, tiled=True), 0, [])
    for a, column in zip(arrays, columns):
        share = whole[..., at : at + column.shape[along]]
        finished.append(share.reshape(*share.shape[:along], *a.shape[along:]))
        at += column.shape[along]
    return tuple(finished)


def taken_together(value, axis):
    everything = from_everyone(value, axis)
    return jnp.sum(everything.astype(jnp.float32), axis=0)


def sent_together(arrays, axis, dim, along):
    widths = [a.shape[along] for a in arrays]
    both = jnp.concatenate(arrays, axis=along)
    whole = lax.psum_scatter(both, axis, scatter_dimension=dim, tiled=True)
    return tuple(jnp.split(whole, [sum(widths[:k]) for k in range(1, len(widths))], axis=along))


def of_everyone(value, axis):
    return from_everyone(value, axis).sum(axis=0)


def together(arrays, axis):
    flat, at, finished = (jnp.concatenate([a.reshape(-1) for a in arrays]), 0, [])
    subtotal = of_everyone(flat, axis)
    for a in arrays:
        finished.append(subtotal[at : at + a.size].reshape(a.shape))
        at += a.size
    return tuple(finished)


def summed_on_arrival(value, axis, dim):
    count = lax.axis_size(axis)
    tiles = lax.all_to_all(split_up(value, dim, count), axis, 0, 0, tiled=True)
    return jnp.sum(tiles.astype(jnp.float32), axis=0)


def in_one_piece_3(arrays, axis, dim, along):
    widths = [math.prod(a.shape[along:]) for a in arrays]
    both = jnp.concatenate(
        [a.reshape(*a.shape[:along], w) for a, w in zip(arrays, widths)], axis=along
    )
    whole = summed_on_arrival(both, axis, dim)
    tiles = jnp.split(whole, [sum(widths[:k]) for k in range(1, len(widths))], axis=along)
    return tuple((b.reshape(*whole.shape[:along], *a.shape[along:]) for a, b in zip(arrays, tiles)))


def rms_scale(values):
    return lax.rsqrt(jnp.mean(values * values, axis=-1, keepdims=True) + epsilon)


def rotary_tables(length):
    half_dim = HD // 2
    inverse = 10000.0 ** (-(jnp.arange(half_dim).astype(jnp.float32) * 2.0) / HD)
    angles = jnp.arange(length).astype(jnp.float32)[:, None] * inverse[None, :]
    return (jnp.cos(angles)[:, None, :], jnp.sin(angles)[:, None, :])


def rotate(values, cosine_table, sine_table, direction):
    half_dim = HD // 2
    leading = values[..., :half_dim]
    trailing = values[..., half_dim:]
    sine_signed = sine_table * direction
    return jnp.concatenate(
        [
            leading * cosine_table - trailing * sine_signed,
            trailing * cosine_table + leading * sine_signed,
        ],
        axis=-1,
    )


def group_rows(rows_local):
    return gather_directly(rows_local, "tensor", 0)


def local_sums(term_fn, row_count):
    return sent_and_summed(term_fn(jnp.int32(0), row_count * lax.axis_size("tensor")), "tensor", 0)


def slicer(source_rows):

    def term_fn(offset, extent):
        return source_rows

    return term_fn


def gather_weights(
    attn_gain,
    moe_gain,
    router_weight,
    query_weight,
    key_weight,
    value_weight,
    output_weight,
    expert_gate,
    expert_up,
    expert_down,
):
    small_set = turned_gather((attn_gain, moe_gain, router_weight), "dp", (0, 0, 0))
    attention_set = in_one_piece(
        (query_weight, key_weight, value_weight, output_weight), "dp", 0, 1
    )
    expert_set = (
        lax.all_gather(expert_gate, "dp", axis=1, tiled=True),
        lax.all_gather(expert_up, "dp", axis=1, tiled=True),
        lax.all_gather(expert_down, "dp", axis=1, tiled=True),
    )
    return (small_set, attention_set, expert_set)


def expert_slots(routes, capacity):
    flat_ids = routes.reshape(-1)
    assignments = flat_ids.shape[0]
    sorted_order = jnp.argsort(flat_ids, stable=True)
    picked = (flat_ids[:, None] == jnp.arange(E, dtype=jnp.int32)[None, :]).astype(jnp.int32)
    counts = jnp.sum(picked, axis=0)
    starts = jnp.cumsum(counts) - counts
    sorted_ids = flat_ids[sorted_order]
    slot_sorted = jnp.arange(assignments, dtype=jnp.int32) - starts[sorted_ids]
    slot_ranks = jnp.zeros((assignments,), jnp.int32).at[sorted_order].set(slot_sorted)
    destination = flat_ids * capacity + slot_ranks
    owners = jnp.arange(assignments, dtype=jnp.int32) // TOPK
    source = jnp.full((E * capacity,), routes.shape[0], jnp.int32).at[destination].set(owners)
    return (destination, source)


def block_layout(length):
    block_rows = min(512, length)
    return (block_rows, length // block_rows)


def attention_scores(query_block, key_rot, segment_block, position_block, segments, positions):
    scores = jnp.einsum(
        "qgrd,kgd->grqk", query_block, key_rot, preferred_element_type=jnp.float32
    ) * HD ** (-0.5)
    allowed = (segment_block[:, None] == segments[None, :]) & (
        position_block[:, None] >= positions[None, :]
    )
    return jnp.where(allowed, scores, masked_score)


def attention_core(query_rot, key_rot, value_all, segments):
    length, local_kv, group_size = (query_rot.shape[0], query_rot.shape[1], query_rot.shape[2])
    block_rows, block_count = block_layout(length)
    positions = jnp.arange(length, dtype=jnp.int32)

    def one_block(pieces):
        query_block, segment_block, position_block = pieces
        scores = attention_scores(
            query_block, key_rot, segment_block, position_block, segments, positions
        )
        row_max = jnp.max(scores, axis=-1, keepdims=True)
        exponent = jnp.exp(scores - row_max)
        row_total = jnp.sum(exponent, axis=-1, keepdims=True)
        softmax_out = (exponent / row_total).astype(jnp.bfloat16)
        context = jnp.einsum(
            "grqk,kgd->qgrd", softmax_out, value_all, preferred_element_type=jnp.float32
        )
        log_total = (row_max + jnp.log(row_total))[..., 0]
        return (
            context.astype(jnp.bfloat16).reshape(block_rows, local_kv * group_size * HD),
            log_total,
        )

    contexts, log_totals = lax.map(
        one_block,
        (
            query_rot.reshape(block_count, block_rows, local_kv, group_size, HD),
            segments.reshape(block_count, block_rows),
            positions.reshape(block_count, block_rows),
        ),
    )
    return (contexts.reshape(length, local_kv * group_size * HD), log_totals)


def attention_backward(query_rot, key_rot, value_all, segments, log_totals, context_grad):
    length, local_kv, group_size = (query_rot.shape[0], query_rot.shape[1], query_rot.shape[2])
    block_rows, block_count = block_layout(length)
    positions = jnp.arange(length, dtype=jnp.int32)
    score_scale = HD ** (-0.5)

    def one_block(running, pieces):
        key_total, value_total = running
        query_block, segment_block, position_block, log_block, grad_block = pieces
        scores = attention_scores(
            query_block, key_rot, segment_block, position_block, segments, positions
        )
        softmax_out = jnp.exp(scores - log_block[..., None])
        grad_heads = grad_block.reshape(block_rows, local_kv, group_size, HD)
        prob_grad = jnp.einsum(
            "qgrd,kgd->grqk", grad_heads, value_all, preferred_element_type=jnp.float32
        )
        centre = jnp.sum(prob_grad * softmax_out, axis=-1, keepdims=True)
        score_grad = (softmax_out * (prob_grad - centre)).astype(jnp.bfloat16)
        query_grad = (
            jnp.einsum("grqk,kgd->qgrd", score_grad, key_rot, preferred_element_type=jnp.float32)
            * score_scale
        )
        key_total = (
            key_total
            + jnp.einsum(
                "grqk,qgrd->kgd", score_grad, query_block, preferred_element_type=jnp.float32
            )
            * score_scale
        )
        value_total = value_total + jnp.einsum(
            "grqk,qgrd->kgd",
            softmax_out.astype(jnp.bfloat16),
            grad_heads,
            preferred_element_type=jnp.float32,
        )
        return ((key_total, value_total), query_grad)

    zero_rows = jnp.zeros((length, local_kv, HD), jnp.float32)
    pieces = (
        query_rot.reshape(block_count, block_rows, local_kv, group_size, HD),
        segments.reshape(block_count, block_rows),
        positions.reshape(block_count, block_rows),
        log_totals,
        context_grad.reshape(block_count, block_rows, local_kv * group_size * HD),
    )
    (key_total, value_total), query_grads = lax.scan(one_block, (zero_rows, zero_rows), pieces)
    return (query_grads.reshape(length, local_kv * group_size, HD), key_total, value_total)


def attention_forward(hidden, gain_full, attention_set, segments, tables):
    query_w, key_w, value_w, output_w = attention_set
    length = segments.shape[0]
    local_heads = query_w.shape[1] // HD
    local_kv = key_w.shape[1] // HD
    cosine_table, sine_table = tables
    normed = (hidden * rms_scale(hidden) * gain_full.astype(jnp.float32)).astype(jnp.bfloat16)
    normed_all = group_rows(normed)
    query_pre = jnp.dot(normed_all, query_w, preferred_element_type=jnp.float32).reshape(
        length, local_heads, HD
    )
    query_rot = (
        rotate(query_pre, cosine_table, sine_table, 1.0)
        .astype(jnp.bfloat16)
        .reshape(length, local_kv, local_heads // local_kv, HD)
    )
    key_pre = jnp.dot(normed_all, key_w, preferred_element_type=jnp.float32).reshape(
        length, local_kv, HD
    )
    key_rot = rotate(key_pre, cosine_table, sine_table, 1.0).astype(jnp.bfloat16)
    value_all = (
        jnp.dot(normed_all, value_w, preferred_element_type=jnp.float32)
        .astype(jnp.bfloat16)
        .reshape(length, local_kv, HD)
    )
    context, log_totals = attention_core(query_rot, key_rot, value_all, segments)

    def project(offset, extent):
        return lax.dot_general(context, output_w, contract_last, preferred_element_type=jnp.float32)

    middle = hidden + local_sums(project, hidden.shape[0])
    return (middle, (normed_all, query_rot, key_rot, value_all, context, log_totals))


def moe_front(middle, gain_full, router_full, expert_set, routes_all, source):
    gate_w, up_w, down_w = expert_set
    normed = (middle * rms_scale(middle) * gain_full.astype(jnp.float32)).astype(jnp.bfloat16)
    normed_all = group_rows(normed)
    logits = jnp.dot(normed_all, router_full, preferred_element_type=jnp.float32)
    route_mask = (routes_all[:, :, None] == jnp.arange(E, dtype=jnp.int32)[None, None, :]).astype(
        jnp.float32
    )
    chosen = jnp.sum(route_mask * logits[:, None, :], axis=-1)
    gating = jax.nn.softmax(chosen, axis=-1)
    expert_in = jnp.take(normed_all, source, axis=0, mode="fill", fill_value=0).reshape(E, -1, D)
    gate_pre = jnp.einsum("ecd,edf->ecf", expert_in, gate_w, preferred_element_type=jnp.float32)
    up_pre = jnp.einsum("ecd,edf->ecf", expert_in, up_w, preferred_element_type=jnp.float32)
    activation = (jax.nn.silu(gate_pre) * up_pre).astype(jnp.bfloat16)
    expert_out = jnp.einsum("ecf,edf->ecd", activation, down_w, preferred_element_type=jnp.float32)
    return (normed_all, route_mask, gating, expert_in, gate_pre, up_pre, activation, expert_out)


def norm_grad(values, gain_full, normed_grad):
    row_scale = rms_scale(values)
    unit_rows = values * row_scale
    weighted = normed_grad * gain_full.astype(jnp.float32)
    input_grad = row_scale * (
        weighted - unit_rows * jnp.mean(weighted * unit_rows, axis=-1, keepdims=True)
    )
    return (input_grad, jnp.sum(normed_grad * unit_rows, axis=0))


def on_device(
    hidden_in,
    out_grad,
    attn_gain,
    query_weight,
    key_weight,
    value_weight,
    output_weight,
    moe_gain,
    router_weight,
    expert_gate,
    expert_up,
    expert_down,
    expert_ids,
    segment_ids,
):
    tensor_size = lax.axis_size("tensor")
    tensor_rank = lax.axis_index("tensor")
    row_count = hidden_in.shape[0]
    length = row_count * tensor_size
    capacity = length * TOPK * 5 // (4 * E)
    segments, routes_all = in_one_piece_2((segment_ids, expert_ids), "tensor", 0, 1)
    destination, source = expert_slots(routes_all, capacity)
    tables = rotary_tables(length)
    small_set, attention_set, expert_set = gather_weights(
        attn_gain,
        moe_gain,
        router_weight,
        query_weight,
        key_weight,
        value_weight,
        output_weight,
        expert_gate,
        expert_up,
        expert_down,
    )
    hidden = hidden_in.astype(jnp.float32)
    middle, unused = attention_forward(hidden, small_set[0], attention_set, segments, tables)
    moe_state = moe_front(middle, small_set[1], small_set[2], expert_set, routes_all, source)
    gating, expert_out = (moe_state[2], moe_state[7])
    slot_gate = (
        jnp.zeros((E * capacity,), jnp.float32).at[destination].set(gating.reshape(length * TOPK))
    )
    mixture = (
        jnp.zeros((length + 1, D), jnp.float32)
        .at[source]
        .add(expert_out.reshape(E * capacity, D) * slot_gate[:, None])[:length]
    )
    block_out = (middle + local_sums(slicer(mixture), row_count)).astype(jnp.bfloat16)
    anchored = lax.optimization_barrier(
        (
            hidden_in,
            attn_gain,
            moe_gain,
            router_weight,
            query_weight,
            key_weight,
            value_weight,
            output_weight,
            expert_gate,
            expert_up,
            expert_down,
            block_out,
        )
    )
    small_again, attention_again, expert_again = (small_set, attention_set, expert_set)
    hidden_again = anchored[0].astype(jnp.float32)
    middle, recorded = attention_forward(
        hidden_again, small_again[0], attention_again, segments, tables
    )
    normed_moe, route_mask, gating, expert_in, gate_pre, up_pre, activation, expert_out = moe_front(
        middle, small_again[1], small_again[2], expert_again, routes_all, source
    )
    normed_attn, query_rot, key_rot, value_all, context, log_totals = recorded
    query_w, key_w, value_w, output_w = attention_again
    gate_w, up_w, down_w = expert_again
    cosine_table, sine_table = tables
    out_grad_all = group_rows(out_grad)
    grad_slots = jnp.take(out_grad_all, source, axis=0, mode="fill", fill_value=0).reshape(
        E, capacity, D
    )
    slot_dot = jnp.einsum("ecd,ecd->ec", expert_out, grad_slots, preferred_element_type=jnp.float32)
    gate_local = slot_dot.reshape(E * capacity)[destination].reshape(length, TOPK)
    gate_grad = taken_together(gate_local.astype(jnp.bfloat16), "tensor").astype(jnp.float32)
    chosen_grad = gating * (gate_grad - jnp.sum(gating * gate_grad, axis=-1, keepdims=True))
    logit_grad = jnp.sum(route_mask * chosen_grad[:, :, None], axis=1).astype(jnp.bfloat16)
    router_grad = lax.dot_general(
        normed_moe, logit_grad, contract_rows, preferred_element_type=jnp.float32
    )
    slot_gate = (
        jnp.zeros((E * capacity,), jnp.float32).at[destination].set(gating.reshape(length * TOPK))
    )
    out_slots = (slot_gate.reshape(E, capacity, 1) * grad_slots).astype(jnp.bfloat16)
    act_grad = jnp.einsum("ecd,edf->ecf", out_slots, down_w, preferred_element_type=jnp.float32)
    down_w_grad = jnp.einsum(
        "ecd,ecf->edf", out_slots, activation, preferred_element_type=jnp.float32
    )
    sig_gate = jax.nn.sigmoid(gate_pre)
    gate_pre_grad = (act_grad * up_pre * sig_gate * (1.0 + gate_pre * (1.0 - sig_gate))).astype(
        jnp.bfloat16
    )
    up_pre_grad = (act_grad * gate_pre * sig_gate).astype(jnp.bfloat16)
    gate_w_grad = jnp.einsum(
        "ecd,ecf->edf", expert_in, gate_pre_grad, preferred_element_type=jnp.float32
    )
    up_w_grad = jnp.einsum(
        "ecd,ecf->edf", expert_in, up_pre_grad, preferred_element_type=jnp.float32
    )
    input_grad = jnp.einsum(
        "ecf,edf->ecd", gate_pre_grad, gate_w, preferred_element_type=jnp.float32
    ) + jnp.einsum("ecf,edf->ecd", up_pre_grad, up_w, preferred_element_type=jnp.float32)
    normed_moe_all = (
        jnp.zeros((length + 1, D), jnp.float32)
        .at[source]
        .add(input_grad.reshape(E * capacity, D))[:length]
    )
    expert_grads = tuple(
        (
            part.astype(jnp.float32)
            for part in sent_together(
                (
                    gate_w_grad.astype(jnp.bfloat16),
                    up_w_grad.astype(jnp.bfloat16),
                    down_w_grad.astype(jnp.bfloat16),
                ),
                "dp",
                1,
                0,
            )
        )
    )
    local_logit = lax.dynamic_slice_in_dim(logit_grad, tensor_rank * row_count, row_count, 0)
    router_part = lax.dot_general(
        local_logit, small_again[2], contract_last, preferred_element_type=jnp.float32
    )
    normed_moe_grad = local_sums(slicer(normed_moe_all), row_count) + router_part
    middle_grad, moe_gain_grad = norm_grad(middle, small_again[1], normed_moe_grad)
    middle_grad = middle_grad + out_grad.astype(jnp.float32)
    attn_grad_all = group_rows(middle_grad.astype(jnp.bfloat16))
    context_grad = jnp.dot(attn_grad_all, output_w, preferred_element_type=jnp.float32).astype(
        jnp.bfloat16
    )
    output_w_grad = lax.dot_general(
        attn_grad_all, context, contract_rows, preferred_element_type=jnp.float32
    )
    query_total, key_total, value_total = attention_backward(
        query_rot, key_rot, value_all, segments, log_totals, context_grad
    )
    query_grad = (
        rotate(query_total, cosine_table, sine_table, -1.0).astype(jnp.bfloat16).reshape(length, -1)
    )
    key_grad = (
        rotate(key_total, cosine_table, sine_table, -1.0).astype(jnp.bfloat16).reshape(length, -1)
    )
    value_grad = value_total.astype(jnp.bfloat16).reshape(length, -1)
    query_w_grad = lax.dot_general(
        normed_attn, query_grad, contract_rows, preferred_element_type=jnp.float32
    )
    key_w_grad = lax.dot_general(
        normed_attn, key_grad, contract_rows, preferred_element_type=jnp.float32
    )
    value_w_grad = lax.dot_general(
        normed_attn, value_grad, contract_rows, preferred_element_type=jnp.float32
    )
    attention_grads = tuple(
        (
            part.astype(jnp.float32)
            for part in sent_together(
                (
                    query_w_grad.astype(jnp.bfloat16),
                    key_w_grad.astype(jnp.bfloat16),
                    value_w_grad.astype(jnp.bfloat16),
                    output_w_grad.astype(jnp.bfloat16),
                ),
                "dp",
                0,
                1,
            )
        )
    )

    def input_term(offset, extent):
        summed = lax.dot_general(
            query_grad, query_w, contract_last, preferred_element_type=jnp.float32
        )
        summed = summed + lax.dot_general(
            key_grad, key_w, contract_last, preferred_element_type=jnp.float32
        )
        return summed + lax.dot_general(
            value_grad, value_w, contract_last, preferred_element_type=jnp.float32
        )

    normed_attn_grad = local_sums(input_term, row_count)
    hidden_norm_grad, attn_gain_grad = norm_grad(hidden_again, small_again[0], normed_attn_grad)
    hidden_grad = middle_grad + hidden_norm_grad
    gain_totals = together((attn_gain_grad, moe_gain_grad), "tensor")
    small_grads = (
        summed_on_arrival(gain_totals[0].astype(jnp.bfloat16), "dp", 0),
        *in_one_piece_3(
            (gain_totals[1].astype(jnp.bfloat16), router_grad.astype(jnp.bfloat16)), "dp", 0, 1
        ),
    )
    return (
        block_out,
        hidden_grad,
        small_grads[0],
        attention_grads[0],
        attention_grads[1],
        attention_grads[2],
        attention_grads[3],
        small_grads[1],
        small_grads[2],
        expert_grads[0],
        expert_grads[1],
        expert_grads[2],
    )


def solution(mesh):
    return jax.shard_map(
        on_device,
        mesh=mesh,
        in_specs=(
            P(("dp", "tensor"), None),
            P(("dp", "tensor"), None),
            P("dp"),
            P("dp", "tensor"),
            P("dp", "tensor"),
            P("dp", "tensor"),
            P("dp", "tensor"),
            P("dp"),
            P("dp", None),
            P(None, "dp", "tensor"),
            P(None, "dp", "tensor"),
            P(None, "dp", "tensor"),
            P(("dp", "tensor"), None),
            P(("dp", "tensor")),
        ),
        out_specs=(
            P(("dp", "tensor"), None),
            P(("dp", "tensor"), None),
            P("dp"),
            P("dp", "tensor"),
            P("dp", "tensor"),
            P("dp", "tensor"),
            P("dp", "tensor"),
            P("dp"),
            P("dp", None),
            P(None, "dp", "tensor"),
            P(None, "dp", "tensor"),
            P(None, "dp", "tensor"),
        ),
        check_vma=False,
    )
```

profile of v0, /device:TPU:0, one launch (start us, length us, event | category | flops | bytes accessed | tf_op | source)
XLA Modules:
  0.0 1944.7 jit_solution(6643614009539246013)
XLA Ops:
  12.4 98.2 %all_gather.19 = bf16[1024,34]{1,0:T(8,128)(2,1)S(1)} all-gather(bf16[32,34]{1,0:T(8,128)(2,1)S(1)} %pad_maximum_fusion.7), channel_id=1, replica_groups=mesh['dp'=32,'tensor'=4] {'dp'}, dimensions={0}, use_global_device_ids=true | all-gather | bytes 71808 | tf_op jit(solution)/shard_map/all_gather | solution.py:53
  119.3 29.6 %all_gather.18 = s32[1024,9]{0,1:T(8,128)S(1)} all-gather(s32[256,9]{0,1:T(8,128)S(1)} %pad_add_fusion), channel_id=1, replica_groups=mesh['dp'=32,'tensor'=4] {'tensor'}, dimensions={0}, use_global_device_ids=true | all-gather | bytes 46080 | tf_op jit(solution)/shard_map/all_gather | solution.py:73
  160.4 22.2 %while.39 = (s32[]{:T(128)}, bf16[2,512,256]{2,1,0:T(8,128)(2,1)S(1)}, s32[2,512]{1,0:T(2,128)S(1)}, s32[1024,1]{0,1:T(1,128)S(1)}, s32[2,512]{1,0:T(2,128)S(1)}...) while((s32[]{:T(128)}, ...), condition=%wide.region_4.5_spmd.clone, body=%wide.region_1.4_spmd.clone.sunk | while | flops 551158784 | bytes 19955816 | solution.py:241
  192.6 6.8 sort.17
  199.3 45.5 %gather_fusion = s32[8192]{0:T(1024)S(1)} fusion(s32[8192]{0:T(1024)S(1)} %reshape.539, s32[8192]{0:T(1024)S(1)} %get-tuple-element.571), kind=kCustom, calls=%fused_computation.3 | custom fusion | bytes 98304 | tf_op jit(solution)/shard_map/gather | solution.py:194
  261.8 15.9 select_subtract_fusion
  277.7 30.5 %scatter_custom_fusion = s32[8192]{0:T(1024)S(1)} fusion(s32[8192]{0:T(1024)S(1)} %get-tuple-element.572, s32[8192]{0:T(1024)S(1)} %select_subtract_fusion, s32[]{:T(128)} %constant.100.clone.1), kind=kCustom, calls=%fused_computation.292 | custom fusion | bytes 32772 | tf_op jit(solution)/shard_map/scatter | solution.py:196
  308.8 30.5 %scatter_custom_fusion.1 = s32[10240]{0:T(1024)S(1)} fusion(s32[8192]{0:T(1024)S(1)} %get-tuple-element.531, s32[8192]{0:T(1024)S(1)} %add_select_fusion, s32[]{:T(128)} %constant.140.clone.1), kind=kCustom, calls=%fused_computation.285 | custom fusion | bytes 40964 | tf_op jit(solution)/shard_map/scatter | solution.py:199
  339.4 44.0 %gather_fusion.2 = bf16[10240,1024]{1,0:T(8,128)(2,1)} fusion(bf16[1024,1024]{1,0:T(8,128)(2,1)S(1)} %bitcast.389, s32[10240]{0:T(1024)S(1)} %get-tuple-element.569), kind=kCustom, calls=%fused_computation.clone | custom fusion | bytes 41984000 | tf_op jit(solution)/shard_map/jit(_take)/gather | solution.py:346
  384.9 30.9 %scatter_custom_fusion.2 = f32[10240]{0:T(1024)S(1)} fusion(s32[8192]{0:T(1024)S(1)} %get-tuple-element.531, f32[8192]{0:T(1024)S(1)} %reshape.663, f32[]{:T(128)} %constant.133.clone.1), kind=kCustom, calls=%fused_computation.283 | custom fusion | bytes 40964 | tf_op jit(solution)/shard_map/scatter | solution.py:405
  415.8 17.4 broadcast_select_fusion.2
  433.2 13.7 fusion.174
  446.9 28.2 %fusion.95 = f32[32,320,1024]{2,1,0:T(8,128)} fusion(bf16[32,1024,128]{2,1,0:T(8,128)(2,1)} %all-gather.11.cloned.1.call-done, f32[32,320,128]{2,1,0:T(8,128)} %fusion.174, bf16[32,320,1024]{2,1,0:T(8,128)(2,1)} %bitcast.399, bf16[32,1024,128]{2,1,0:T(8,128)(2,1)} %all-gather.9.cloned.1.call-done), kind=kOutput, calls=%fused_computation.124 | convolution fusion | flops 5376573440 | bytes 84934656 | tf_op jit(solution)/shard_map/ecf,edf->ecd/dot_general | solution.py:350
  475.2 28.2 %bitcast_multiply_fusion.1 = f32[10240,1024]{1,0:T(8,128)} fusion(f32[32,320,1024]{2,1,0:T(8,128)} %fusion.95, f32[10240]{0:T(1024)S(1)} %scatter_custom_fusion.2), kind=kLoop, calls=%fused_computation.107 | loop fusion | flops 10485760 | bytes 83927040 | tf_op jit(solution)/shard_map/mul | solution.py:410
  503.3 90.4 %scatter_custom_fusion.3 = f32[1025,1024]{1,0:T(8,128)} fusion(s32[10240]{0:T(1024)S(1)} %get-tuple-element.570, f32[10240,1024]{1,0:T(8,128)} %bitcast_multiply_fusion.1, f32[]{:T(128)} %constant.133.clone.1), kind=kCustom, calls=%fused_computation.129 | custom fusion | flops 10485760 | bytes 4198912 | tf_op jit(solution)/shard_map/scatter-add | solution.py:410
  596.0 51.7 %all_to_all.77 = f32[4,256,1024]{2,1,0:T(8,128)} all-to-all(f32[4,256,1024]{2,1,0:T(8,128)S(1)} %bitcast.412), channel_id=1, replica_groups=mesh['dp'=32,'tensor'=4] {'tensor'}, dimensions={0} | all-to-all | bytes 8388608 | tf_op jit(solution)/shard_map/all_to_all | solution.py:45
  657.5 25.6 %all-to-all-done.4 = bf16[4,256,1024]{2,1,0:T(8,128)(2,1)S(1)} async-done(((bf16[4,256,1024]{2,1,0:T(8,128)(2,1)}), bf16[4,256,1024]{2,1,0:T(8,128)(2,1)S(1)}, u32[]{:S(2)}, u32[]{:S(2)}) %all-to-all-start.4) | async-done | bytes 2097184 | tf_op jit(solution)/shard_map/all_to_all | solution.py:22
  694.1 15.6 while.40
  712.0 51.7 %all_to_all.78 = f32[4,256,1024]{2,1,0:T(8,128)} all-to-all(f32[4,256,1024]{2,1,0:T(8,128)S(1)} %fusion.117), channel_id=1, replica_groups=mesh['dp'=32,'tensor'=4] {'tensor'}, dimensions={0} | all-to-all | bytes 8388608 | tf_op jit(solution)/shard_map/all_to_all | solution.py:45
  775.7 19.1 all-to-all-done.7
  800.6 52.4 %gather_fusion.3 = bf16[10240,1024]{1,0:T(8,128)(2,1)} fusion(bf16[1024,1024]{1,0:T(8,128)(2,1)} %bitcast.391, s32[10240]{0:T(1024)S(1)} %copy-done.49), kind=kCustom, calls=%fused_computation.1.clone | custom fusion | bytes 41984000 | tf_op jit(solution)/shard_map/jit(_take)/gather | solution.py:442
  853.8 44.0 %gather_fusion.4 = bf16[10240,1024]{1,0:T(8,128)(2,1)} fusion(bf16[1024,1024]{1,0:T(8,128)(2,1)S(1)} %bitcast.387, s32[10240]{0:T(1024)S(1)} %copy-done.49), kind=kCustom, calls=%fused_computation.2.clone | custom fusion | bytes 41984000 | tf_op jit(solution)/shard_map/jit(_take)/gather | solution.py:346
  898.0 28.2 %broadcast_select_fusion.1 = (bf16[10240,1024]{1,0:T(8,128)(2,1)}, bf16[10240,1024]{1,0:T(8,128)(2,1)}) fusion(bf16[10240,1024]{1,0:T(8,128)(2,1)} %gather_fusion.3, pred[10240]{0:T(1024)(128)(4,1)S(1)} %copy-done.73, bf16[10240,1024]{1,0:T(8,128)(2,1)} %gather_fusion.4), kind=kLoop, calls=%fused_computation.110 | loop fusion | flops 20971520 | bytes 83896320 | tf_op jit(solution)/shard_map/jit(_take)/select_n | solution.py:442
  926.2 13.9 fusion.177
  940.1 15.8 multiply_convert_fusion
  956.0 12.0 fusion.87
  968.1 50.7 %gather_fusion.1 = bf16[8192]{0:T(1024)(128)(2,1)S(1)} fusion(bf16[10240]{0:T(1024)(128)(2,1)S(1)} %reshape.554, s32[8192]{0:T(1024)S(1)} %copy-done.66), kind=kCustom, calls=%fused_computation.4 | custom fusion | bytes 65536 | tf_op jit(solution)/shard_map/gather | solution.py:446
  1027.8 31.0 %scatter_custom_fusion.4 = f32[10240]{0:T(1024)S(1)} fusion(s32[8192]{0:T(1024)} %copy-done.75, f32[8192]{0:T(1024)S(1)} %reshape.679, f32[]{:T(128)} %constant.133.clone.1), kind=kCustom, calls=%fused_computation.281 | custom fusion | bytes 41472 | tf_op jit(solution)/shard_map/scatter | solution.py:454
  1058.9 17.4 multiply_convert_fusion.1
  1076.3 19.3 fusion.178
  1095.5 32.1 %convolution_add_fusion = f32[32,320,1024]{2,1,0:T(8,128)} fusion(f32[32,320,1024]{2,1,0:T(8,128)} %fusion.178, bf16[32,320,128]{2,1,0:T(8,128)(2,1)} %get-tuple-element.546, bf16[32,1024,128]{2,1,0:T(8,128)(2,1)} %all-gather.9.cloned.1.call-done), kind=kOutput, calls=%fused_computation.114 | convolution fusion | flops 2694840320 | bytes 94896128 | tf_op jit(solution)/shard_map/ecf,edf->ecd/dot_general | solution.py:474
  1127.7 90.7 %scatter_custom_fusion.5 = f32[1025,1024]{1,0:T(8,128)} fusion(s32[10240]{0:T(1024)} %copy-done.74, f32[10240,1024]{1,0:T(8,128)} %bitcast.400, f32[]{:T(128)} %constant.133.clone.1), kind=kCustom, calls=%fused_computation.127 | custom fusion | flops 10485760 | bytes 4198912 | tf_op jit(solution)/shard_map/scatter-add | solution.py:478
  1228.2 15.5 fusion.92
  1243.8 32.5 %all-to-all-done.8 = f32[4,256,1024]{2,1,0:T(8,128)} async-done(((f32[4,256,1024]{2,1,0:T(8,128)}), f32[4,256,1024]{2,1,0:T(8,128)}, u32[]{:S(2)}, u32[]{:S(2)}) %all-to-all-start.8) | async-done | bytes 4194336 | tf_op jit(solution)/shard_map/all_to_all | solution.py:45
  1290.0 13.9 convolution_convert_fusion.1
  1304.0 11.7 all-to-all-done.10
  1318.9 73.7 %while.41 = (s32[]{:T(128)}, f32[1024,2,64]{0,2,1:T(8,128)S(1)}, f32[1024,2,64]{0,2,1:T(8,128)}, f32[2,512,2,2,64]{1,0,4,3,2:T(2,128)}, bf16[2,512,2,2,64]{1,4,3...) while((s32[]{:T(128)}, f32[1024,2,64]{0,2,1:T(8,128)S(1)}, ...), condition=%wide.region_37.39_spmd.clone, body=%wide.region_35.38_spmd.clone.sunk | while | flops 1375991808 | bytes 120922456 | solution.py:298
  1324.5 5.6 fusion.279
  1336.7 10.4 dynamic_update_slice.29
  1361.2 5.6 fusion.279
  1373.5 10.4 dynamic_update_slice.29
  1405.5 13.5 convolution_convert_fusion
  1419.0 17.7 pad_maximum_fusion
  1448.2 49.2 %all-to-all-done.11 = f32[4,256,1024]{2,1,0:T(8,128)} async-done(((f32[4,256,1024]{2,1,0:T(8,128)}), f32[4,256,1024]{2,1,0:T(8,128)}, u32[]{:S(2)}, u32[]{:S(2)}) %all-to-all-start.11) | async-done | bytes 4194336 | tf_op jit(solution)/shard_map/all_to_all | solution.py:45
  1504.5 122.5 %reduce-scatter.7.cloned.1.call-done = bf16[32,768]{1,0:T(8,128)(2,1)} async-done(((bf16[1024,768]{1,0:T(8,128)(2,1)}), bf16[32,768]{1,0:T(8,128)(2,1)}) %reduce-scatter.7.cloned.1.call-update) | async-done | bytes 49168
  1642.4 8.5 all-to-all-done.13
  1655.3 9.6 all-to-all-done.14
  1666.7 268.4 %reduce-scatter.5.cloned.1.call-done = bf16[96,32,128]{2,1,0:T(8,128)(2,1)} async-done(((bf16[96,1024,128]{2,1,0:T(8,128)(2,1)}), bf16[96,32,128]{2,1,0:T(8,128)(2,1)}) %reduce-scatter.5.cloned.1.call-update) | async-done | bytes 786448 | tf_op jit(solution)/shard_map/reduce_scatter | solution.py:89
  (442 shorter events, 267.2 us)
Async XLA Ops:
  7.2 112.1 %copy-start.85 = (s32[256]{0:T(256)S(1)}, s32[256]{0:T(256)}, u32[]{:S(2)}) copy-start(s32[256]{0:T(256)} %param.35) | copy-start | bytes 3076
  7.2 112.1 %copy-start.84 = (s32[256,8]{0,1:T(8,128)S(1)}, s32[256,8]{0,1:T(8,128)}, u32[]{:S(2)}) copy-start(s32[256,8]{0,1:T(8,128)} %param.34) | copy-start | bytes 24580
  7.2 143.0 %all-gather.5.cloned.1.call-start = ((), (), s32[]{:S(2)}) async-start(), calls=%async_computation.17 | async-start | bytes 1622016 | tf_op jit(solution)/shard_map/all_gather | solution.py:66
  8.7 424.5 %all-gather.7.cloned.1.call-start = ((), (), s32[]{:S(2)}) async-start(), calls=%async_computation.18 | async-start | bytes 8650752 | tf_op jit(solution)/shard_map/all_gather | solution.py:180
  9.4 437.5 %all-gather.11.cloned.1.call-start = ((), (), s32[]{:S(2)}) async-start(), calls=%async_computation.20 | async-start | bytes 8650752 | tf_op jit(solution)/shard_map/all_gather | solution.py:182
  110.7 272.7 %copy-start.20 = (bf16[1024,34]{1,0:T(8,128)(2,1)}, bf16[1024,34]{1,0:T(8,128)(2,1)S(1)}, u32[]{:S(2)}) copy-start(bf16[1024,34]{1,0:T(8,128)(2,1)S(1)} %all_gather.19) | copy-start | bytes 208900
  111.0 144.7 %copy-start.62 = (f32[1024]{0:T(1024)}, f32[1024]{0:T(1024)S(1)}, u32[]{:S(2)}) copy-start(f32[1024]{0:T(1024)S(1)} %get-tuple-element.444) | copy-start | bytes 12292
  115.1 39.1 %all-to-all-start = ((bf16[4,256,1024]{2,1,0:T(8,128)(2,1)}), bf16[4,256,1024]{2,1,0:T(8,128)(2,1)S(1)}, u32[]{:S(2)}, u32[]{:S(2)}) async-start(bf16[4,256,1024]{2,1,0:T(8,128)(2,1)} %broadcast_in_dim.81), calls=%async_computation | async-start | bytes 4194304 | tf_op jit(solution)/shard_map/all_to_all | solution.py:22
  118.7 328.2 %all-gather.9.cloned.1.call-start = ((), (), s32[]{:S(2)}) async-start(), calls=%async_computation.19 | async-start | bytes 8650752 | tf_op jit(solution)/shard_map/all_gather | solution.py:181
  186.5 66.2 %all-to-all-start.1 = ((f32[4,256,1024]{2,1,0:T(8,128)}), f32[4,256,1024]{2,1,0:T(8,128)}, u32[]{:S(2)}, u32[]{:S(2)}) async-start(f32[4,256,1024]{2,1,0:T(8,128)} %fusion.119), calls=%async_computation.1 | async-start | bytes 8388608 | tf_op jit(solution)/shard_map/all_to_all | solution.py:45
  191.6 192.5 %copy-start.45 = (s32[1024,8]{0,1:T(8,128)}, s32[1024,8]{0,1:T(8,128)S(1)}, u32[]{:S(2)}) copy-start(s32[1024,8]{0,1:T(8,128)S(1)} %slice.136) | copy-start | bytes 98308
  257.5 81.9 %all-to-all-start.2 = ((bf16[4,256,1024]{2,1,0:T(8,128)(2,1)}), bf16[4,256,1024]{2,1,0:T(8,128)(2,1)S(1)}, u32[]{:S(2)}, u32[]{:S(2)}) async-start(bf16[4,256,1024]{2,1,0:T(8,128)(2,1)} %broadcast_in_dim.86), calls=%async_computation.2 | async-start | bytes 4194304 | tf_op jit(solution)/shard_map/all_to_all | solution.py:22
  308.8 76.0 %copy-start.75 = (s32[8192]{0:T(1024)}, s32[8192]{0:T(1024)S(1)}, u32[]{:S(2)}) copy-start(s32[8192]{0:T(1024)S(1)} %get-tuple-element.531) | copy-start | bytes 98308
  339.3 76.4 %copy-start.72 = (pred[10240]{0:T(1024)(128)(4,1)}, pred[10240]{0:T(1024)(128)(4,1)S(1)}, u32[]{:S(2)}) copy-start(pred[10240]{0:T(1024)(128)(4,1)S(1)} %compare_and_fusion) | copy-start | bytes 30724
  339.4 164.0 %copy-start.74 = (s32[10240]{0:T(1024)}, s32[10240]{0:T(1024)S(1)}, u32[]{:S(2)}) copy-start(s32[10240]{0:T(1024)S(1)} %get-tuple-element.570) | copy-start | bytes 122884
  596.0 54.4 %copy-start.16 = (f32[256,1024]{1,0:T(8,128)S(1)}, f32[256,1024]{1,0:T(8,128)}, u32[]{:S(2)}) copy-start(f32[256,1024]{1,0:T(8,128)} %copy-done.15) | copy-start | bytes 3145732
  653.5 29.6 %all-to-all-start.4 = ((bf16[4,256,1024]{2,1,0:T(8,128)(2,1)}), bf16[4,256,1024]{2,1,0:T(8,128)(2,1)S(1)}, u32[]{:S(2)}, u32[]{:S(2)}) async-start(bf16[4,256,1024]{2,1,0:T(8,128)(2,1)} %broadcast_in_dim.88), calls=%async_computation.4 | async-start | bytes 4194304 | tf_op jit(solution)/shard_map/all_to_all | solution.py:22
  709.7 54.0 %copy-start.11 = (bf16[1024,2,64]{0,2,1:T(8,128)(2,1)}, bf16[1024,2,64]{0,2,1:T(8,128)(2,1)S(1)}, u32[]{:S(2)}) copy-start(bf16[1024,2,64]{0,2,1:T(8,128)(2,1)S(1)} %get-tuple-element.928) | copy-start | bytes 786436
  709.7 54.0 %copy-start.17 = (bf16[2,512,2,2,64]{1,4,3,2,0:T(8,128)(2,1)}, bf16[2,512,2,2,64]{1,4,3,2,0:T(8,128)(2,1)S(1)}, u32[]{:S(2)}) copy-start(bf16[2,512,2,2,64]{1,4,3,2,0:T(8,128)(2,1)S(1)} %get-tuple-element.936) | copy-start | bytes 1572868
  709.7 54.0 %copy-start.39 = (bf16[2,512,256]{2,1,0:T(8,128)(2,1)}, bf16[2,512,256]{2,1,0:T(8,128)(2,1)S(1)}, u32[]{:S(2)}) copy-start(bf16[2,512,256]{2,1,0:T(8,128)(2,1)S(1)} %get-tuple-element.187) | copy-start | bytes 1572868
  709.7 54.0 %copy-start.67 = (f32[2,2,2,512]{3,2,1,0:T(2,128)}, f32[2,2,2,512]{3,2,1,0:T(2,128)S(1)}, u32[]{:S(2)}) copy-start(f32[2,2,2,512]{3,2,1,0:T(2,128)S(1)} %get-tuple-element.882) | copy-start | bytes 49156
  711.9 51.8 %copy-start.29 = (bf16[256,1024]{1,0:T(8,128)(2,1)S(1)}, bf16[256,1024]{1,0:T(8,128)(2,1)}, u32[]{:S(2)}) copy-start(bf16[256,1024]{1,0:T(8,128)(2,1)} %param.23) | copy-start | bytes 1572868
  765.3 29.4 %all-to-all-start.7 = ((bf16[4,256,1024]{2,1,0:T(8,128)(2,1)}), bf16[4,256,1024]{2,1,0:T(8,128)(2,1)S(1)}, u32[]{:S(2)}, u32[]{:S(2)}) async-start(bf16[4,256,1024]{2,1,0:T(8,128)(2,1)} %broadcast_in_dim.90), calls=%async_computation.7 | async-start | bytes 4194304 | tf_op jit(solution)/shard_map/all_to_all | solution.py:22
  796.7 56.2 %all-to-all-start.6 = ((bf16[4,256,1024]{2,1,0:T(8,128)(2,1)}), bf16[4,256,1024]{2,1,0:T(8,128)(2,1)S(1)}, u32[]{:S(2)}, u32[]{:S(2)}) async-start(bf16[4,256,1024]{2,1,0:T(8,128)(2,1)} %broadcast_in_dim.89), calls=%async_computation.6 | async-start | bytes 4194304 | tf_op jit(solution)/shard_map/all_to_all | solution.py:22
  800.6 52.4 %copy-start.21 = (bf16[1024,34]{1,0:T(8,128)(2,1)S(1)}, bf16[1024,34]{1,0:T(8,128)(2,1)}, u32[]{:S(2)}) copy-start(bf16[1024,34]{1,0:T(8,128)(2,1)} %copy-done.20) | copy-start | bytes 208900
  853.0 44.9 %copy-start = (bf16[4,256,1024]{2,1,0:T(8,128)(2,1)}, bf16[4,256,1024]{2,1,0:T(8,128)(2,1)S(1)}, u32[]{:S(2)}) copy-start(bf16[4,256,1024]{2,1,0:T(8,128)(2,1)S(1)} %all-to-all-done.6) | copy-start | bytes 6291460
  853.7 44.3 %copy-start.73 = (pred[10240]{0:T(1024)(128)(4,1)S(1)}, pred[10240]{0:T(1024)(128)(4,1)}, u32[]{:S(2)}) copy-start(pred[10240]{0:T(1024)(128)(4,1)} %copy-done.72) | copy-start | bytes 30724
  1019.9 7.4 all-to-all-start.9
  1223.1 53.2 %all-to-all-start.8 = ((f32[4,256,1024]{2,1,0:T(8,128)}), f32[4,256,1024]{2,1,0:T(8,128)}, u32[]{:S(2)}, u32[]{:S(2)}) async-start(f32[4,256,1024]{2,1,0:T(8,128)} %bitcast.414), calls=%async_computation.8 | async-start | bytes 8388608 | tf_op jit(solution)/shard_map/all_to_all | solution.py:45
  1228.2 51.8 %copy-start.54 = (bf16[1024,32]{0,1:T(8,128)(2,1)}, bf16[1024,32]{0,1:T(8,128)(2,1)S(1)}, u32[]{:S(2)}) copy-start(bf16[1024,32]{0,1:T(8,128)(2,1)S(1)} %select_reduce_fusion) | copy-start | bytes 196612
  1285.5 30.2 %all-to-all-start.10 = ((bf16[4,256,1024]{2,1,0:T(8,128)(2,1)}), bf16[4,256,1024]{2,1,0:T(8,128)(2,1)}, u32[]{:S(2)}, u32[]{:S(2)}) async-start(bf16[4,256,1024]{2,1,0:T(8,128)(2,1)} %broadcast_in_dim.94), calls=%async_computation.10 | async-start | bytes 4194304 | tf_op jit(solution)/shard_map/all_to_all | solution.py:22
  1289.9 337.1 %reduce-scatter.7.cloned.1.call-start = ((), (), s32[]{:S(2)}) async-start(), calls=%async_computation.22 | async-start | bytes 1622016
  1318.9 77.0 %copy-start.28 = (f32[1024,32]{0,1:T(8,128)S(1)}, f32[1024,32]{0,1:T(8,128)}, u32[]{:S(2)}) copy-start(f32[1024,32]{0,1:T(8,128)} %copy-done.26) | copy-start | bytes 393220
  1318.9 76.9 %copy-start.41 = (f32[1024,32]{0,1:T(8,128)S(1)}, f32[1024,32]{0,1:T(8,128)}, u32[]{:S(2)}) copy-start(f32[1024,32]{0,1:T(8,128)} %get-tuple-element.575) | copy-start | bytes 393220
  1405.5 529.6 %reduce-scatter.5.cloned.1.call-start = ((), (), s32[]{:S(2)}) async-start(), calls=%async_computation.21 | async-start | bytes 25952256 | tf_op jit(solution)/shard_map/reduce_scatter | solution.py:89
  1442.3 55.0 %all-to-all-start.11 = ((f32[4,256,1024]{2,1,0:T(8,128)}), f32[4,256,1024]{2,1,0:T(8,128)}, u32[]{:S(2)}, u32[]{:S(2)}) async-start(f32[4,256,1024]{2,1,0:T(8,128)} %bitcast.413), calls=%async_computation.11 | async-start | bytes 8388608 | tf_op jit(solution)/shard_map/all_to_all | solution.py:45
  1447.4 52.7 %copy-start.6 = (bf16[256,1024]{1,0:T(8,128)(2,1)S(1)}, bf16[256,1024]{1,0:T(8,128)(2,1)}, u32[]{:S(2)}) copy-start(bf16[256,1024]{1,0:T(8,128)(2,1)} %param.22) | copy-start | bytes 1572868
  1447.4 52.7 %copy-start.71 = (f32[1024]{0:T(1024)S(1)}, f32[1024]{0:T(1024)}, u32[]{:S(2)}) copy-start(f32[1024]{0:T(1024)} %copy-done.69) | copy-start | bytes 12292
  1447.5 52.7 %copy-start.80 = (f32[256]{0:T(256)S(1)}, f32[256]{0:T(256)}, u32[]{:S(2)}) copy-start(f32[256]{0:T(256)} %copy-done.79) | copy-start | bytes 3076
  1447.5 53.1 %copy-start.81 = (f32[1024]{0:T(1024)S(1)}, f32[1024]{0:T(1024)}, u32[]{:S(2)}) copy-start(f32[1024]{0:T(1024)} %get-tuple-element.439) | copy-start | bytes 12292
  1447.5 180.3 %copy-start.31 = (bf16[256,1024]{1,0:T(8,128)(2,1)S(1)}, bf16[256,1024]{1,0:T(8,128)(2,1)}, u32[]{:S(2)}) copy-start(bf16[256,1024]{1,0:T(8,128)(2,1)} %param.23) | copy-start | bytes 1572868
  1447.5 180.3 %copy-start.65 = (f32[1024]{0:T(1024)S(1)}, f32[1024]{0:T(1024)}, u32[]{:S(2)}) copy-start(f32[1024]{0:T(1024)} %copy-done.62) | copy-start | bytes 12292
  1447.5 180.3 %copy-start.78 = (f32[256]{0:T(256)S(1)}, f32[256]{0:T(256)}, u32[]{:S(2)}) copy-start(f32[256]{0:T(256)} %copy-done.76) | copy-start | bytes 3076
  1447.5 180.3 %copy-start.83 = (f32[256]{0:T(256)S(1)}, f32[256]{0:T(256)}, u32[]{:S(2)}) copy-start(f32[256]{0:T(256)} %copy-done.82) | copy-start | bytes 3076
  1448.0 179.8 %copy-start.8 = (f32[256,1024]{1,0:T(8,128)S(1)}, f32[256,1024]{1,0:T(8,128)}, u32[]{:S(2)}) copy-start(f32[256,1024]{1,0:T(8,128)} %reduce_sum.259) | copy-start | bytes 3145732
  1501.2 133.4 %all-to-all-start.12 = ((f32[4,1,2048]{2,1,0:T(1,128)}), f32[4,1,2048]{2,1,0:T(1,128)S(1)}, u32[]{:S(2)}, u32[]{:S(2)}) async-start(f32[4,1,2048]{2,1,0:T(1,128)} %broadcast_in_dim.95), calls=%async_computation.12 | async-start | bytes 65536 | tf_op jit(solution)/shard_map/all_to_all | solution.py:22
  1635.8 15.1 all-to-all-start.13
  1650.9 14.0 all-to-all-start.14
  (69 other events, 898.0 us)
Sparse Core Ops, SparseCore 0:
  11.7 71.1 all-gather.4
  85.6 107.1 all-gather.6
  195.6 122.0 all-gather.10
  320.3 102.1 all-gather.8
  1405.6 221.3 reduce-scatter.6
  1633.6 301.4 reduce-scatter.4
where the time goes:
time: 1960 us; the launch traced here: 1940 us
  waiting for transfers between devices  553 us (28%)
  local copies, waits for them, and re-layouts  437 us (22%)
  other arithmetic  356 us (18%)
  matrix products  297 us (15%)
  blocking collectives  231 us (12%)
  starting transfers between devices  54.4 us (3%)
    reduce_scatter x1, waiting for transfers between devices, sent_together(): whole = lax.psum_scatter(both, axis, scatter_dimension=dim, tiled=True)  268 us
    unnamed x7, waiting for transfers between devices  124 us
    all_to_all x2, blocking collectives, sent_and_summed(): lax.all_to_all(tiles, axis, split_axis=0, concat_axis=0, tiled=True)  103 us
    all_gather x1, blocking collectives, turned_gather(): whole = lax.all_gather(both, axis, axis=0, tiled=True)  98.2 us
    scatter-add x1, other arithmetic, on_device(): normed_moe_all = jnp.zeros((length + 1, D), jnp.float32).at[source].add(i...  90.7 us
    scatter-add x1, other arithmetic, on_device(): mixture = jnp.zeros((length + 1, D), jnp.float32).at[source].add(expert_o...  90.4 us
    gather x2, local copies, waits for them, and re-layouts, moe_front(): jnp.take(normed_all, source, axis=0, mode='fill', fill_value=0)  88 us
    all_to_all x3, waiting for transfers between devices, sent_and_summed(): lax.all_to_all(tiles, axis, split_axis=0, concat_axis=0, tiled=True)  81.7 us
  transfers between devices with their start and end apart: 19, of which 10 were waited for; matrix products, arithmetic and copies ran while one was open for 22% of the time, Pallas kernels for 0%

commit v1 on v0

v1 whole, which is shorter than its diff:
```python
import functools

import jax
import jax.numpy as jnp
import numpy as np
from jax import lax
from jax.experimental import pallas as pl
from jax.experimental.pallas import tpu as pltpu
from jax.sharding import Mesh
from jax.sharding import PartitionSpec as P

D = 1024
HD = 64
E = 32
SEQ = 1024
LOCAL = 256
HEADS = 4
QUAD = 4
FF = 128
F = QUAD * FF
EPS = 1e-06
MASKED = -1e30
BLOCK = 256
TOKENS = 2048
STEPS = 4

DP = ("x", "z", "yh")
TENSOR = ("yl", "core")
RING = ("yh", "yl", "core")
PLANE = ("x", "z")
ALL = ("x", "z", "yh", "yl", "core")

F32 = jnp.float32
BF = jnp.bfloat16
LAST = (((1,), (1,)), ((), ()))
MIB = 1024 * 1024
MESH = pl.DeviceIdType.MESH
SMALL = 896


def mm(a, b):
    return jnp.dot(a, b, preferred_element_type=F32)


def mm_last(a, b):
    return lax.dot_general(a, b, LAST, preferred_element_type=F32)


class Place:
    def __init__(self):
        self.x = lax.axis_index("x")
        self.z = lax.axis_index("z")
        self.yh = lax.axis_index("yh")
        self.yl = lax.axis_index("yl")
        self.core = lax.axis_index("core")
        self.y = self.yh * 2 + self.yl

    def chip(self, k):
        return lax.rem(self.y + k, 4)

    def ring(self, k):
        chip = self.chip(k)
        return {"yh": chip // 2, "yl": lax.rem(chip, 2)}

    def along(self, axis, k):
        return {axis: lax.rem(getattr(self, axis) + k, 4)}

    def sibling(self):
        return {"core": 1 - self.core}

    def partner(self):
        return {"yl": 1 - self.yl}

    def diagonal(self):
        return {"yl": 1 - self.yl, "core": 1 - self.core}

    def opposite(self):
        return {"yh": 1 - self.yh}


def greet(devices):
    barrier = pltpu.get_barrier_semaphore()
    for device in devices:
        pl.semaphore_signal(barrier, inc=1, device_id=device, device_id_type=MESH)
    pl.semaphore_wait(barrier, len(devices))


def push(src, dst, send, recv, i, device):
    copy = pltpu.make_async_remote_copy(
        src_ref=src, dst_ref=dst, send_sem=send.at[i], recv_sem=recv.at[i],
        device_id=device, device_id_type=MESH,
    )
    copy.start()
    return copy


def keep(src, dst, sem):
    copy = pltpu.make_async_copy(src, dst, sem)
    copy.start()
    return copy


class RingGather:
    def __init__(self, at, own, out, send, recv, here, base=0):
        self.at, self.out, self.send, self.recv, self.base = at, out, send, recv, base
        self.half = own.shape[0] // 2
        me = out.at[self.slot(0)]
        self.kept = keep(own, me, here)
        self.copies = {}
        self.go(1, own, me, at.ring(1))
        self.go(2, own, me, at.ring(3))
        self.go(0, own, me, at.sibling())

    def slot(self, k):
        return self.at.chip(k) * 2 + self.at.core

    def go(self, i, src, dst, device):
        self.copies[i] = push(src, dst, self.send, self.recv, self.base + i, device)

    def pass_on(self, i, view, device):
        self.go(i, view, view, device)

    def forward(self):
        lo, hi = pl.ds(0, self.half), pl.ds(self.half, self.half)
        self.copies[1].wait_recv()
        self.pass_on(3, self.out.at[self.slot(3), lo], self.at.ring(1))
        self.pass_on(4, self.out.at[self.slot(3)], self.at.sibling())
        self.copies[2].wait_recv()
        self.pass_on(5, self.out.at[self.slot(1), hi], self.at.ring(3))
        self.pass_on(6, self.out.at[self.slot(1)], self.at.sibling())

    def forward_far(self):
        lo, hi = pl.ds(0, self.half), pl.ds(self.half, self.half)
        self.copies[3].wait_recv()
        self.pass_on(7, self.out.at[self.slot(2), lo], self.at.sibling())
        self.copies[5].wait_recv()
        self.pass_on(8, self.out.at[self.slot(2), hi], self.at.sibling())

    def finish(self):
        for i in (0, 4, 6, 7, 8):
            self.copies[i].wait_recv()
        for i in range(9):
            self.copies[i].wait_send()
        self.kept.wait()


def gather_ring_kernel(count, *refs):
    owns, outs = refs[:count], refs[count : 2 * count]
    send, recv, here = refs[2 * count :]
    at = Place()
    greet([at.sibling(), at.ring(1), at.ring(3)])
    gathers = [
        RingGather(at, own, out, send, recv, here.at[i], 9 * i)
        for i, (own, out) in enumerate(zip(owns, outs))
    ]
    for gather in gathers:
        gather.forward()
    for gather in gathers:
        gather.forward_far()
    for gather in gathers:
        gather.finish()


def gather_ring(owns, ident):
    count = len(owns)
    hbm = pl.BlockSpec(memory_space=pl.ANY)
    outs = pl.pallas_call(
        functools.partial(gather_ring_kernel, count),
        in_specs=[hbm] * count,
        out_specs=[hbm] * count,
        out_shape=[jax.ShapeDtypeStruct((8, *own.shape), own.dtype) for own in owns],
        scratch_shapes=[
            pltpu.SemaphoreType.DMA((9 * count,)),
            pltpu.SemaphoreType.DMA((9 * count,)),
            pltpu.SemaphoreType.DMA((count,)),
        ],
        compiler_params=pltpu.CompilerParams(collective_id=ident, has_side_effects=True),
        name="gather_ring",
    )(*owns)
    return [out.reshape(-1, out.shape[-1]) for out in outs]


class PairGather:
    def __init__(self, at, own, out, send, recv, here, base, pieces):
        self.at, self.out, self.send, self.recv, self.base = at, out, send, recv, base
        size = own.shape[0] // pieces
        self.parts = [pl.ds(i * size, size) for i in range(pieces)]
        me = at.yl * 2 + at.core
        self.other = (1 - at.yl) * 2 + at.core
        self.kept = keep(own, out.at[me], here)
        self.far = [
            push(own.at[part], out.at[me, part], send, recv, base + 1 + i, at.partner())
            for i, part in enumerate(self.parts)
        ]
        self.near = [push(own, out.at[me], send, recv, base, at.sibling())]

    def forward(self):
        for i, part in enumerate(self.parts):
            self.far[i].wait_recv()
            view = self.out.at[self.other, part]
            index = self.base + 1 + len(self.parts) + i
            self.near.append(push(view, view, self.send, self.recv, index, self.at.sibling()))

    def finish(self):
        for copy in self.near:
            copy.wait_recv()
        for copy in (*self.far, *self.near):
            copy.wait_send()
        self.kept.wait()


PIECES = 4


def gather_pair_kernel(own, out, send, recv, here):
    at = Place()
    greet([at.sibling(), at.partner()])
    gather = PairGather(at, own, out, send, recv, here, 0, PIECES)
    gather.forward()
    gather.finish()


def gather_pair(own, ident):
    hbm = pl.BlockSpec(memory_space=pl.ANY)
    out = pl.pallas_call(
        gather_pair_kernel,
        in_specs=[hbm],
        out_specs=hbm,
        out_shape=jax.ShapeDtypeStruct((4, *own.shape), own.dtype),
        scratch_shapes=[
            pltpu.SemaphoreType.DMA((1 + 2 * PIECES,)),
            pltpu.SemaphoreType.DMA((1 + 2 * PIECES,)),
            pltpu.SemaphoreType.DMA,
        ],
        compiler_params=pltpu.CompilerParams(collective_id=ident, has_side_effects=True),
        name="gather_pair",
    )(own)
    return out.reshape(-1, own.shape[1])


def startup_kernel(hidden, segment, small, hidden_all, segment_all, small_all, send, recv, here):
    at = Place()
    greet(
        [
            at.sibling(), at.partner(), at.diagonal(), at.opposite(),
            at.along("z", 1), at.along("z", 3), at.along("x", 1), at.along("x", 3),
        ]
    )
    rank = at.yl * 2 + at.core
    first = (at.x * 4 + at.z) * 2
    mine = small_all.at[first + at.yh]
    shared = keep(small, mine, here.at[0])
    to_opposite = push(small, mine, send, recv, 0, at.opposite())
    gather = PairGather(at, hidden, hidden_all, send, recv, here.at[1], 12, PIECES)
    seg_here = keep(segment, segment_all.at[rank], here.at[2])
    seg_copies = [
        push(segment, segment_all.at[rank], send, recv, 9 + i, device)
        for i, device in enumerate((at.sibling(), at.partner(), at.diagonal()))
    ]
    copies = [to_opposite]

    def ring(axis, base, view, step, low, high):
        up = push(view(0), view(0), send, recv, base, at.along(axis, 1))
        down = push(view(0), view(0), send, recv, base + 1, at.along(axis, 3))
        up.wait_recv()
        far_up = push(low(3), low(3), send, recv, base + 2, at.along(axis, 1))
        down.wait_recv()
        far_down = push(high(1), high(1), send, recv, base + 3, at.along(axis, 3))
        far_up.wait_recv()
        far_down.wait_recv()
        copies.extend([up, down, far_up, far_down])

    shared.wait()
    to_opposite.wait_recv()
    z_at = lambda k: (at.x * 4 + lax.rem(at.z + k, 4)) * 2
    ring(
        "z", 1, lambda k: small_all.at[pl.ds(z_at(k), 2)], 2,
        lambda k: small_all.at[pl.ds(z_at(k), 1)],
        lambda k: small_all.at[pl.ds(z_at(k) + 1, 1)],
    )
    gather.forward()
    x_at = lambda k: lax.rem(at.x + k, 4) * 8
    ring(
        "x", 5, lambda k: small_all.at[pl.ds(x_at(k), 8)], 8,
        lambda k: small_all.at[pl.ds(x_at(k), 4)],
        lambda k: small_all.at[pl.ds(x_at(k) + 4, 4)],
    )
    gather.finish()
    seg_here.wait()
    for copy in seg_copies:
        copy.wait_recv()
    for copy in (*copies, *seg_copies):
        copy.wait_send()


def startup(hidden, segment, small, ident):
    hbm = pl.BlockSpec(memory_space=pl.ANY)
    sems = 12 + 1 + 2 * PIECES
    hidden_all, segment_all, small_all = pl.pallas_call(
        startup_kernel,
        in_specs=[hbm] * 3,
        out_specs=[hbm] * 3,
        out_shape=[
            jax.ShapeDtypeStruct((4, *hidden.shape), hidden.dtype),
            jax.ShapeDtypeStruct((4, *segment.shape), segment.dtype),
            jax.ShapeDtypeStruct((32, *small.shape), small.dtype),
        ],
        scratch_shapes=[
            pltpu.SemaphoreType.DMA((sems,)),
            pltpu.SemaphoreType.DMA((sems,)),
            pltpu.SemaphoreType.DMA((3,)),
        ],
        compiler_params=pltpu.CompilerParams(collective_id=ident, has_side_effects=True),
        name="startup",
    )(hidden, segment, small)
    return hidden_all.reshape(SEQ, D), segment_all, small_all.reshape(D, SMALL)


def scatter_ring_kernel(
    part, out, near, half_a, half_b, full_up, full_down, to_far, to_up, to_down, send, recv
):
    at = Place()
    greet([at.sibling(), at.ring(1), at.ring(3)])
    half = out.shape[0] // 2
    lo, hi = pl.ds(0, half), pl.ds(half, half)
    near_copies = {
        k: push(part.at[at.chip(k) * 2 + 1 - at.core], near.at[k], send, recv, k, at.sibling())
        for k in (2, 1, 3, 0)
    }

    def chip_sum(k):
        near_copies[k].wait_recv()
        return part[at.chip(k) * 2 + at.core].astype(F32) + near[k].astype(F32)

    to_far[...] = chip_sum(2).astype(BF)
    far_up = push(to_far.at[lo], half_a, send, recv, 4, at.ring(1))
    far_down = push(to_far.at[hi], half_b, send, recv, 5, at.ring(3))
    total = chip_sum(1)
    far_up.wait_recv()
    to_up[lo, :] = (total[:half] + half_a[...].astype(F32)).astype(BF)
    to_up[hi, :] = total[half:].astype(BF)
    up = push(to_up, full_up, send, recv, 6, at.ring(1))
    total = chip_sum(3)
    far_down.wait_recv()
    to_down[lo, :] = total[:half].astype(BF)
    to_down[hi, :] = (total[half:] + half_b[...].astype(F32)).astype(BF)
    down = push(to_down, full_down, send, recv, 7, at.ring(3))
    out[...] = chip_sum(0)
    up.wait_recv()
    out[...] += full_up[...].astype(F32)
    down.wait_recv()
    out[...] += full_down[...].astype(F32)
    for copy in (*near_copies.values(), far_up, far_down, up, down):
        copy.wait_send()


def scatter_ring(part, ident):
    vmem = pl.BlockSpec(memory_space=pltpu.VMEM)
    rows, columns = part.shape[0] // 8, part.shape[1]
    block, half = pltpu.VMEM((rows, columns), BF), pltpu.VMEM((rows // 2, columns), BF)
    return pl.pallas_call(
        scatter_ring_kernel,
        in_specs=[vmem],
        out_specs=vmem,
        out_shape=jax.ShapeDtypeStruct((rows, columns), F32),
        scratch_shapes=[
            pltpu.VMEM((4, rows, columns), BF), half, half, block, block, block, block, block,
            pltpu.SemaphoreType.DMA((8,)),
            pltpu.SemaphoreType.DMA((8,)),
        ],
        compiler_params=pltpu.CompilerParams(
            collective_id=ident, has_side_effects=True, vmem_limit_bytes=32 * MIB
        ),
        name="scatter_ring",
    )(part.reshape(8, rows, columns))


def scatter_pair_kernel(part, out, near, far, to_far, send, recv):
    at = Place()
    greet([at.sibling(), at.partner()])
    size = out.shape[0] // PIECES
    parts = [pl.ds(i * size, size) for i in range(PIECES)]
    other, own = (1 - at.yl) * 2, at.yl * 2
    first = [
        push(part.at[other + 1 - at.core, rows], near.at[1, rows], send, recv, i, at.sibling())
        for i, rows in enumerate(parts)
    ]
    second = push(part.at[own + 1 - at.core], near.at[0], send, recv, PIECES, at.sibling())
    sent = []
    for i, rows in enumerate(parts):
        first[i].wait_recv()
        total = part[other + at.core, rows, :].astype(F32) + near[1, rows, :].astype(F32)
        to_far[rows, :] = total.astype(BF)
        index = PIECES + 1 + i
        sent.append(push(to_far.at[rows], far.at[rows], send, recv, index, at.partner()))
    second.wait_recv()
    out[...] = part[own + at.core].astype(F32) + near[0].astype(F32)
    for i, rows in enumerate(parts):
        sent[i].wait_recv()
        out[rows, :] += far[rows, :].astype(F32)
    for copy in (*first, second, *sent):
        copy.wait_send()


def scatter_pair(part, ident):
    vmem = pl.BlockSpec(memory_space=pltpu.VMEM)
    rows, columns = part.shape[0] // 4, part.shape[1]
    block = pltpu.VMEM((rows, columns), BF)
    return pl.pallas_call(
        scatter_pair_kernel,
        in_specs=[vmem],
        out_specs=vmem,
        out_shape=jax.ShapeDtypeStruct((rows, columns), F32),
        scratch_shapes=[
            pltpu.VMEM((2, rows, columns), BF), block, block,
            pltpu.SemaphoreType.DMA((1 + 2 * PIECES,)),
            pltpu.SemaphoreType.DMA((1 + 2 * PIECES,)),
        ],
        compiler_params=pltpu.CompilerParams(
            collective_id=ident, has_side_effects=True, vmem_limit_bytes=32 * MIB
        ),
        name="scatter_pair",
    )(part.reshape(4, rows, columns))


def rotary_tables():
    half = HD // 2
    inverse = (10000.0 ** (-(np.arange(half, dtype=np.float64) * 2.0) / HD)).astype(np.float32)
    angles = np.arange(SEQ, dtype=np.float32)[:, None] * inverse[None, :]
    cosine, sine = np.cos(angles), np.sin(angles)
    wide_cosine = np.concatenate([cosine] * 4, axis=1)
    wide_sine = np.concatenate([-sine, sine] * 2, axis=1)
    return wide_cosine.astype(np.float32), wide_sine.astype(np.float32)


def swapped(values):
    lane = lax.broadcasted_iota(jnp.int32, values.shape, 1)
    low = (lane % HD) < HD // 2
    return jnp.where(low, pltpu.roll(values, 96, 1), pltpu.roll(values, 32, 1))


def rotated(values, cosine, sine):
    return values * cosine + swapped(values) * sine


def bias_block(key_segment, query_segment, first, rows):
    key_at = lax.broadcasted_iota(jnp.int32, (rows, BLOCK), 0)
    query_at = lax.broadcasted_iota(jnp.int32, (rows, BLOCK), 1) + first
    allowed = (key_segment == query_segment) & (key_at <= query_at)
    return jnp.where(allowed, 0.0, MASKED)


def attention_forward_kernel(
    hidden, gain, weights, cosine, sine, seg_column, seg_row, out_grad,
    part, normed, query, key, value, context_t, log_total, out_grad_all,
    bias, send, recv, here,
):
    at = Place()
    greet([at.sibling(), at.ring(1), at.ring(3)])
    gather = RingGather(at, out_grad, out_grad_all, send, recv, here)
    for block in range(SEQ // BLOCK):
        rows = slice(block * BLOCK, (block + 1) * BLOCK)
        values = hidden[rows, :].astype(F32)
        scale = lax.rsqrt(jnp.mean(values * values, axis=-1, keepdims=True) + EPS)
        normed[rows, :] = (values * scale * gain[...]).astype(BF)
    for half in range(2):
        columns = slice(half * 128, half * 128 + 128)
        pre = mm(normed[...], weights[:, columns])
        query[:, columns] = (rotated(pre, cosine[...], sine[...]) * 0.125).astype(BF)
    key_pre = mm(normed[...], weights[:, 256:384])
    key[...] = rotated(key_pre, cosine[...], sine[...]).astype(BF)
    value_pre = mm(normed[...], weights[:, 384:512])
    value[...] = value_pre.astype(BF)
    value_t = value_pre.T.astype(BF)
    for block in range(SEQ // BLOCK):
        first, end = block * BLOCK, (block + 1) * BLOCK
        bias[:end, :] = bias_block(seg_column[:end, :], seg_row[:, first:end], first, end)
        for head in range(HEADS):
            kv = slice((head // 2) * HD, (head // 2) * HD + HD)
            own = slice(head * HD, head * HD + HD)
            scores = mm_last(key[:end, kv], query[first:end, own]) + bias[:end, :]
            top = jnp.max(scores, axis=0, keepdims=True)
            powers = jnp.exp(scores - top)
            total = jnp.sum(powers, axis=0, keepdims=True)
            share = (powers * (1.0 / total)).astype(BF)
            context_t[own, first:end] = mm(value_t[kv, :end], share).astype(BF)
            log_total[head : head + 1, first:end] = top + jnp.log(total)
        if block == 2:
            gather.forward()
    gather.forward_far()
    context = context_t[...].T
    for block in range(SEQ // BLOCK):
        rows = slice(block * BLOCK, (block + 1) * BLOCK)
        part[rows, :] = mm_last(context[rows, :], weights[:, 512:768]).astype(BF)
    gather.finish()


def attention_forward(hidden, gain, weights, tables, seg_column, seg_row, out_grad, ident):
    vmem = pl.BlockSpec(memory_space=pltpu.VMEM)
    hbm = pl.BlockSpec(memory_space=pl.ANY)
    return pl.pallas_call(
        attention_forward_kernel,
        in_specs=[vmem] * 7 + [hbm],
        out_specs=[vmem] * 7 + [hbm],
        out_shape=[
            jax.ShapeDtypeStruct((SEQ, D), BF),
            jax.ShapeDtypeStruct((SEQ, D), BF),
            jax.ShapeDtypeStruct((SEQ, HEADS * HD), BF),
            jax.ShapeDtypeStruct((SEQ, 128), BF),
            jax.ShapeDtypeStruct((SEQ, 128), BF),
            jax.ShapeDtypeStruct((HEADS * HD, SEQ), BF),
            jax.ShapeDtypeStruct((8, SEQ), F32),
            jax.ShapeDtypeStruct((8, *out_grad.shape), BF),
        ],
        scratch_shapes=[
            pltpu.VMEM((SEQ, BLOCK), F32),
            pltpu.SemaphoreType.DMA((9,)),
            pltpu.SemaphoreType.DMA((9,)),
            pltpu.SemaphoreType.DMA,
        ],
        compiler_params=pltpu.CompilerParams(
            collective_id=ident, has_side_effects=True, vmem_limit_bytes=56 * MIB
        ),
        name="attention_forward",
    )(hidden, gain, weights, *tables, seg_column, seg_row, out_grad)


def attention_backward_kernel(
    dattn, normed, weights, cosine, sine, seg_column, seg_row,
    query, key, value, context_t, log_total,
    dn1, grads, bias, dcontext, dquery_t, dkey, dvalue, dall, dall_t,
):
    dcontext[...] = mm(dattn[...], weights[:, 512:768]).astype(BF)
    output_grad_t = mm(context_t[...], dattn[...])
    grads[:, 512:768] = output_grad_t.T.astype(BF)
    key_t = key[...].astype(F32).T.astype(BF)
    dkey[...] = jnp.zeros_like(dkey)
    dvalue[...] = jnp.zeros_like(dvalue)
    for block in range(SEQ // BLOCK):
        first, end = block * BLOCK, (block + 1) * BLOCK
        bias[:end, :] = bias_block(seg_column[:end, :], seg_row[:, first:end], first, end)
        for head in range(HEADS):
            kv = slice((head // 2) * HD, (head // 2) * HD + HD)
            own = slice(head * HD, head * HD + HD)
            query_block = query[first:end, own]
            dcontext_block = dcontext[first:end, own]
            scores = mm_last(key[:end, kv], query_block) + bias[:end, :]
            share = jnp.exp(scores - log_total[head : head + 1, first:end])
            dshare = mm_last(value[:end, kv], dcontext_block)
            centre = jnp.sum(share * dshare, axis=0, keepdims=True)
            dscore = (share * (dshare - centre)).astype(BF)
            dquery_t[own, first:end] = mm(key_t[kv, :end], dscore) * 0.125
            dkey[:end, kv] += mm(dscore, query_block)
            dvalue[:end, kv] += mm(share.astype(BF), dcontext_block)
    turn = -sine[...]
    for half in range(2):
        rows = slice(half * 128, half * 128 + 128)
        piece = rotated(dquery_t[rows, :].T, cosine[...], turn)
        dall[:, rows] = piece.astype(BF)
        dall_t[rows, :] = piece.T.astype(BF)
    piece = rotated(dkey[...], cosine[...], turn)
    dall[:, 256:384] = piece.astype(BF)
    dall_t[256:384, :] = piece.T.astype(BF)
    dall[:, 384:512] = dvalue[...].astype(BF)
    dall_t[384:512, :] = dvalue[...].T.astype(BF)
    grads[:, 0:512] = mm(dall_t[...], normed[...]).T.astype(BF)
    for block in range(SEQ // BLOCK):
        rows = slice(block * BLOCK, (block + 1) * BLOCK)
        dn1[rows, :] = mm_last(dall[rows, :], weights[:, 0:512]).astype(BF)


def attention_backward(dattn, normed, weights, tables, seg_column, seg_row, kept):
    vmem = pl.BlockSpec(memory_space=pltpu.VMEM)
    return pl.pallas_call(
        attention_backward_kernel,
        in_specs=[vmem] * 12,
        out_specs=[vmem] * 2,
        out_shape=[
            jax.ShapeDtypeStruct((SEQ, D), BF),
            jax.ShapeDtypeStruct((D, 768), BF),
        ],
        scratch_shapes=[
            pltpu.VMEM((SEQ, BLOCK), F32),
            pltpu.VMEM((SEQ, HEADS * HD), BF),
            pltpu.VMEM((HEADS * HD, SEQ), F32),
            pltpu.VMEM((SEQ, 128), F32),
            pltpu.VMEM((SEQ, 128), F32),
            pltpu.VMEM((SEQ, 512), BF),
            pltpu.VMEM((512, SEQ), BF),
        ],
        compiler_params=pltpu.CompilerParams(vmem_limit_bytes=56 * MIB),
        name="attention_backward",
    )(dattn, normed, weights, *tables, seg_column, seg_row, *kept)


def experts_kernel(
    x_in, d_in, gating, weights, y_out, dx_out, dgate, grads,
    x, d, xt, dt, y, dx, hidden, load, store,
):
    step = pl.program_id(0)
    rows_at_once = 512
    blocks = TOKENS // rows_at_once
    lane = lax.broadcasted_iota(jnp.int32, (rows_at_once, 128), 1)
    own_first = lax.axis_index("yh") * 16 + step * QUAD

    def rows_of(block):
        return pl.ds(pl.multiple_of(block * rows_at_once, rows_at_once), rows_at_once)

    def loads(block):
        rows = rows_of(block)
        return (
            pltpu.make_async_copy(x_in.at[rows], x.at[rows], load.at[block, 0]),
            pltpu.make_async_copy(d_in.at[rows], d.at[rows], load.at[block, 1]),
        )

    def stores(block):
        rows = rows_of(block)
        return (
            pltpu.make_async_copy(x.at[rows], y_out.at[rows], store.at[block, 0]),
            pltpu.make_async_copy(d.at[rows], dx_out.at[rows], store.at[block, 1]),
        )

    @pl.when(step == 0)
    def _():
        for block in range(blocks):
            for copy in loads(block):
                copy.start()
        dgate[...] = jnp.zeros_like(dgate)

    def tokens_block(block, carry):
        rows = rows_of(block)

        @pl.when(step == 0)
        def _():
            for copy in loads(block):
                copy.wait()
            xt[:, rows] = x[rows, :].T
            dt[:, rows] = d[rows, :].T
            y[rows, :] = jnp.zeros((rows_at_once, D), F32)
            dx[rows, :] = jnp.zeros((rows_at_once, D), F32)

        both = mm(x[rows, :], weights[:, 0 : 2 * F])
        gate, up = both[:, :F], both[:, F:]
        dact = mm(d[rows, :], weights[:, 2 * F :])
        turned = pltpu.roll(gating[rows, :], lax.rem(128 - own_first, 128), 1)
        factor = jnp.concatenate(
            [jnp.broadcast_to(turned[:, i : i + 1], (rows_at_once, FF)) for i in range(QUAD)],
            axis=1,
        )
        q = 1.0 / (1.0 + jnp.exp(-gate))
        silu = gate * q
        act = silu * up
        product = act * dact
        sums = dgate[rows, :]
        for i in range(QUAD):
            own = jnp.sum(product[:, i * FF : (i + 1) * FF], axis=1, keepdims=True)
            sums = jnp.where(lane == own_first + i, own, sums)
        dgate[rows, :] = sums
        dact = dact * factor
        hidden[rows, 0:F] = (dact * up * (q + silu * (1.0 - q))).astype(BF)
        hidden[rows, F : 2 * F] = (dact * silu).astype(BF)
        hidden[rows, 2 * F :] = (act * factor).astype(BF)
        y[rows, :] += mm_last(hidden[rows, 2 * F :], weights[:, 2 * F :])
        dx[rows, :] += mm_last(hidden[rows, 0 : 2 * F], weights[:, 0 : 2 * F])

        @pl.when(step == STEPS - 1)
        def _():
            x[rows, :] = y[rows, :].astype(BF)
            d[rows, :] = dx[rows, :].astype(BF)
            for copy in stores(block):
                copy.start()

        return carry

    lax.fori_loop(0, blocks, tokens_block, 0)

    def grads_block(block, carry):
        rows = pl.ds(pl.multiple_of(block * 512, 512), 512)
        grads[rows, 0 : 2 * F] = mm(xt[rows, :], hidden[:, 0 : 2 * F]).astype(BF)
        grads[rows, 2 * F :] = mm(dt[rows, :], hidden[:, 2 * F :]).astype(BF)
        return carry

    lax.fori_loop(0, D // 512, grads_block, 0)

    @pl.when(step == STEPS - 1)
    def _():
        for block in range(blocks):
            for copy in stores(block):
                copy.wait()


def experts(x, d, gating, weights):
    hbm = pl.BlockSpec(memory_space=pl.ANY)
    whole = pl.BlockSpec((TOKENS, 128), lambda step: (0, 0), pipeline_mode=pl.Buffered(1))
    column = pl.BlockSpec((D, 3 * F), lambda step: (0, step))
    return pl.pallas_call(
        experts_kernel,
        grid=(STEPS,),
        in_specs=[hbm, hbm, whole, column],
        out_specs=[hbm, hbm, whole, column],
        out_shape=[
            jax.ShapeDtypeStruct((TOKENS, D), BF),
            jax.ShapeDtypeStruct((TOKENS, D), BF),
            jax.ShapeDtypeStruct((TOKENS, 128), F32),
            jax.ShapeDtypeStruct((D, STEPS * 3 * F), BF),
        ],
        scratch_shapes=[
            pltpu.VMEM((TOKENS, D), BF),
            pltpu.VMEM((TOKENS, D), BF),
            pltpu.VMEM((D, TOKENS), BF),
            pltpu.VMEM((D, TOKENS), BF),
            pltpu.VMEM((TOKENS, D), F32),
            pltpu.VMEM((TOKENS, D), F32),
            pltpu.VMEM((TOKENS, 3 * F), BF),
            pltpu.SemaphoreType.DMA((TOKENS // 512, 2)),
            pltpu.SemaphoreType.DMA((TOKENS // 512, 2)),
        ],
        compiler_params=pltpu.CompilerParams(vmem_limit_bytes=62 * MIB),
        name="experts",
    )(x, d, gating, weights)


def from_everyone(value, axes):
    count = lax.axis_size(axes)
    shown = jnp.broadcast_to(value[None], (count, *value.shape))
    return lax.all_to_all(shown, axes, 0, 0, tiled=True)


def arrived(value, axes):
    count = lax.axis_size(axes)
    tiles = value.reshape(count, -1, *value.shape[1:])
    return lax.all_to_all(tiles, axes, 0, 0, tiled=True)


def summed(value, axes):
    return jnp.sum(arrived(value, axes).astype(F32), axis=0)


def norm_scale(values):
    return lax.rsqrt(jnp.mean(values * values, axis=-1, keepdims=True) + EPS)


def norm_grad(values, gain, dnormed):
    scale = norm_scale(values)
    unit = values * scale
    weighted = dnormed * gain
    dvalues = scale * (weighted - unit * jnp.mean(weighted * unit, axis=-1, keepdims=True))
    return dvalues, jnp.sum(dnormed * unit, axis=0)


def packed_experts(expert_gate, expert_up, expert_down):
    shares = jnp.stack([expert_gate, expert_up, expert_down])
    shares = shares.reshape(3, 2, STEPS, QUAD, 32, FF)
    return shares.transpose(1, 4, 2, 0, 3, 5).reshape(2, 32, STEPS * 3 * F)


def unpacked_experts(tiles):
    tiles = tiles.reshape(2, 32, STEPS, 3, QUAD, FF).transpose(3, 0, 2, 4, 1, 5)
    tiles = tiles.reshape(3, E, 32, FF).astype(F32)
    return tiles[0], tiles[1], tiles[2]


def on_device(
    hidden_in, out_grad, attn_gain, query_weight, key_weight, value_weight, output_weight,
    moe_gain, router_weight, expert_gate, expert_up, expert_down, expert_ids, segment_ids,
):
    halves = packed_experts(expert_gate, expert_up, expert_down)
    halves = lax.all_to_all(halves, "yh", 0, 0, tiled=True)
    expert_weights = lax.all_gather(
        halves.reshape(64, STEPS * 3 * F), PLANE, axis=0, tiled=True
    )
    small = jnp.concatenate(
        [
            query_weight, key_weight, value_weight, output_weight,
            router_weight, attn_gain[:, None], moe_gain[:, None], jnp.zeros((32, 94), BF),
        ],
        axis=1,
    )
    segment = jnp.pad(segment_ids.reshape(2, 128), ((0, 6), (0, 0)))
    hidden_all, segment_all, small = startup(hidden_in, segment, small, 0)
    router = small[:, 768:800]
    attn_gain_all = small[:, 800].astype(F32)
    moe_gain_all = small[:, 801].astype(F32)
    tables = tuple(jnp.asarray(t) for t in rotary_tables())
    segments = segment_all[:, :2].reshape(SEQ)
    seg_column, seg_row = segments[:, None], segments[None, :]

    part, normed_all, *kept, d = attention_forward(
        hidden_all, attn_gain_all[None, :], small, tables, seg_column, seg_row, out_grad, 1
    )
    d = d.reshape(TOKENS, D)
    hidden = hidden_in.astype(F32)
    middle = hidden + scatter_pair(part, 2)
    normed_moe = (middle * norm_scale(middle) * moe_gain_all).astype(BF)
    logits = mm(normed_moe, router)
    named = jnp.any(
        expert_ids[:, :, None] == jnp.arange(E, dtype=jnp.int32)[None, None, :], axis=1
    )
    top = jnp.max(jnp.where(named, logits, -jnp.inf), axis=-1, keepdims=True)
    powers = jnp.where(named, jnp.exp(logits - top), 0.0)
    gating = powers / jnp.sum(powers, axis=-1, keepdims=True)

    x, gating_all = gather_ring([normed_moe, jnp.pad(gating, ((0, 0), (0, 96)))], 3)
    y, dx, dgate, expert_grads = experts(x, d, gating_all, expert_weights)
    expert_grads = lax.psum_scatter(expert_grads, PLANE, scatter_dimension=0, tiled=True)

    sums = scatter_ring(jnp.concatenate([dx, dgate.astype(BF)], axis=1), 4)
    dgate = sums[:, D : D + E]
    dchosen = gating * (dgate - jnp.sum(gating * dgate, axis=-1, keepdims=True))
    dlogits = dchosen.astype(BF)
    dnormed_moe = sums[:, :D] + mm_last(dlogits, router)
    dmiddle, moe_gain_part = norm_grad(middle, moe_gain_all, dnormed_moe)
    dmiddle = dmiddle + out_grad.astype(F32)
    dattn = gather_pair(dmiddle.astype(BF), 5)
    block_out = (middle + summed(y, RING)).astype(BF)
    router_part = lax.dot_general(
        normed_moe, dlogits, (((0,), (0,)), ((), ())), preferred_element_type=F32
    )
    rest = jnp.concatenate(
        [router_part, moe_gain_part[:, None], jnp.zeros((D, 95), F32)], axis=1
    )
    rest = lax.psum_scatter(rest.astype(BF), PLANE, scatter_dimension=0, tiled=True)
    rest = rest.reshape(2, 1, 32, 128)
    rest = jnp.broadcast_to(rest, (2, 4, 32, 128)).reshape(8, 32, 128)
    rest = jnp.sum(lax.all_to_all(rest, RING, 0, 0, tiled=True).astype(F32), axis=0)

    dn1, attention_grads = attention_backward(
        dattn, normed_all, small, tables, seg_column, seg_row, kept
    )
    attention_grads = lax.psum_scatter(attention_grads, PLANE, scatter_dimension=0, tiled=True)
    dhidden, _ = norm_grad(hidden, attn_gain_all, scatter_pair(dn1, 6))
    hidden_grad = dmiddle + dhidden

    expert_grads = unpacked_experts(
        lax.all_to_all(expert_grads.reshape(2, 32, STEPS * 3 * F), "yh", 0, 0, tiled=True)
    )
    attention_grads = lax.all_to_all(attention_grads.reshape(2, 32, 768), "yh", 0, 0, tiled=True)
    attention_grads = jnp.sum(attention_grads.astype(F32), axis=0)
    own_weights = jnp.concatenate([query_weight, key_weight, value_weight], axis=1)
    attn_gain_grad = jnp.sum(own_weights.astype(F32) * attention_grads[:, :512], axis=1)
    attn_gain_grad = jnp.sum(from_everyone(attn_gain_grad[None], TENSOR), axis=(0, 1))
    return (
        block_out,
        hidden_grad,
        attn_gain_grad / attn_gain.astype(F32),
        attention_grads[:, 0:256],
        attention_grads[:, 256:384],
        attention_grads[:, 384:512],
        attention_grads[:, 512:768],
        rest[:, 32],
        rest[:, :32],
        *expert_grads,
    )


def solution(mesh):
    fine = Mesh(np.asarray(mesh.devices).reshape(4, 4, 2, 2, 2), ALL)
    return jax.shard_map(
        on_device,
        mesh=fine,
        in_specs=(
            P(ALL, None),
            P(ALL, None),
            P(DP),
            P(DP, TENSOR),
            P(DP, TENSOR),
            P(DP, TENSOR),
            P(DP, TENSOR),
            P(DP),
            P(DP, None),
            P(None, DP, TENSOR),
            P(None, DP, TENSOR),
            P(None, DP, TENSOR),
            P(ALL, None),
            P(ALL),
        ),
        out_specs=(
            P(ALL, None),
            P(ALL, None),
            P(DP),
            P(DP, TENSOR),
            P(DP, TENSOR),
            P(DP, TENSOR),
            P(DP, TENSOR),
            P(DP),
            P(DP, None),
            P(None, DP, TENSOR),
            P(None, DP, TENSOR),
            P(None, DP, TENSOR),
        ),
        check_vma=False,
    )
```

time: 1960 us -> 607 us (0.31)
  local copies, waits for them, and re-layouts: 437 us -> 15.6 us
  waiting for transfers between devices: 553 us -> 168 us
  other arithmetic: 356 us -> 18.8 us
  Pallas kernels: 0 us -> 336 us
  matrix products: 297 us -> 3.12 us
  blocking collectives: 231 us -> 22.8 us
  starting transfers between devices: 54.4 us -> 17.8 us
    pallas_call x0 -> x9, Pallas kernels: none -> 336 us  [the longest x1 98.5 us: experts(): pl.pallas_call(experts_kernel, grid=(STEPS,), in_specs=[hbm, hbm, whole,...]
    dot_general x47 -> x3, matrix products: 286 us -> 3.12 us  [the longest x1 1.45 us: mm_last(): return lax.dot_general(a, b, LAST, preferred_element_type=F32)]
    gather x7 -> x0, local copies, waits for them, and re-layouts: 238 us -> none  [the longest x2 88 us: moe_front(): jnp.take(normed_all, source, axis=0, mode='fill', fill_value=0)]
    scatter-add x2 -> x0, other arithmetic: 181 us -> none  [the longest x1 90.7 us: on_device(): normed_moe_all = jnp.zeros((length + 1, D), jnp.float32).at[source].add(i...]
    all_to_all x13 -> x4, waiting for transfers between devices: 160 us -> 14.7 us  [the longest x1 9.17 us: on_device(): lax.all_to_all(expert_grads.reshape(2, 32, STEPS * 3 * F), 'yh', 0, 0, ti...]
    all_gather x2 -> x0, blocking collectives: 128 us -> none  [the longest x1 98.2 us: turned_gather(): whole = lax.all_gather(both, axis, axis=0, tiled=True)]
    unnamed x7 -> x4, waiting for transfers between devices: 124 us -> 0.57 us
    scatter x4 -> x0, local copies, waits for them, and re-layouts: 123 us -> none  [the longest x2 61.9 us: on_device(): jnp.zeros((E * capacity,), jnp.float32).at[destination]]
  transfers between devices with their start and end apart: 19 -> 8, of which waited for: 10 -> 5; matrix products, arithmetic and copies ran while one was open for 22% -> 4% of each run, Pallas kernels for 0% -> 29%
where the time goes in v1:
time: 607 us; the launch traced here: 597 us
  Pallas kernels  336 us (55%)
  waiting for transfers between devices  168 us (28%)
  blocking collectives  22.8 us (4%)
  other arithmetic  18.8 us (3%)
  starting transfers between devices  17.8 us (3%)
  local copies, waits for them, and re-layouts  15.6 us (3%)
  between operations  14.4 us (2%)
    pallas_call x1, Pallas kernels, experts(): pl.pallas_call(experts_kernel, grid=(STEPS,), in_specs=[hbm, hbm, whole,...  98.5 us
    pallas_call x2, Pallas kernels, scatter_pair(): pl.pallas_call(scatter_pair_kernel, in_specs=[vmem], out_specs=vmem, out_...  75.2 us
    reduce_scatter x1, waiting for transfers between devices, on_device(): lax.psum_scatter(attention_grads, PLANE, scatter_dimension=0, tiled=True)  72.8 us
    reduce_scatter x1, waiting for transfers between devices, on_device(): lax.psum_scatter(rest.astype(BF), PLANE, scatter_dimension=0, tiled=True)  70.9 us
    pallas_call x1, Pallas kernels, startup(): pl.pallas_call(startup_kernel, in_specs=[hbm] * 3, out_specs=[hbm] * 3, o...  41.3 us
    pallas_call x1, Pallas kernels, attention_forward(): pl.pallas_call(attention_forward_kernel, in_specs=[vmem] * 7 + [hbm], out...  28.5 us
    pallas_call x1, Pallas kernels, scatter_ring(): pl.pallas_call(scatter_ring_kernel, in_specs=[vmem], out_specs=vmem, out_...  27.6 us
    pallas_call x1, Pallas kernels, gather_ring(): pl.pallas_call(functools.partial(gather_ring_kernel, count), in_specs=[hb...  26.9 us
  transfers between devices with their start and end apart: 8, of which 5 were waited for; matrix products, arithmetic and copies ran while one was open for 4% of the time, Pallas kernels for 29%

profile of v1, /device:TPU:0, one launch (start us, length us, event | category | flops | bytes accessed | tf_op | source)
XLA Modules:
  0.0 596.5 jit_solution(16082787619917986848)
XLA Ops:
  7.2 1.2 maximum_bitcast_fusion
  8.4 0.4 copy.62
  8.9 0.6 reshape.152
  9.5 16.7 %all_to_all.30 = bf16[2,32,6144]{2,1,0:T(8,128)(2,1)} all-to-all(bf16[2,32,6144]{2,1,0:T(8,128)(2,1)S(1)} %reshape.152), channel_id=1, replica_groups=mesh['x'=4,'z'=4,'yh'=2,'yl'=2,'core'=2] {'yh'}, dimensions={0} | all-to-all | bytes 1572864 | tf_op jit(solution)/shard_map/all_to_all | solution.py:768
  26.6 0.6 pad.8.segment
  27.2 0.7 concatenate.14.small
  27.9 41.3 %startup.1 = (bf16[4,256,1024]{2,1,0:T(8,128)(2,1)}, s32[4,8,128]{2,1,0:T(8,128)}, bf16[32,32,896]{2,1,0:T(8,128)(2,1)}) custom-call(bf16[256,1024]{1,0:T(8,128)(2,1)} %hidden.1, s32[8,128]{1,0:T(8,128)} %pad.8.segment, bf16[32,896]{1,0:T(8,128)(2,1)} %concatenate.14.small), custom_call_target="tpu_custom_call" | custom-call | tf_op jit(solution)/shard_map/startup/pallas_call | solution.py:299
  69.2 0.7 slice.52
  70.0 1.0 copy.59.seg_column
  71.0 2.0 convert_reduce_fusion.1
  73.0 28.5 %attention_forward.1 = (bf16[1024,1024]{1,0:T(8,128)(2,1)}, bf16[1024,1024]{1,0:T(8,128)(2,1)}, bf16[1024,256]{1,0:T(8,128)(2,1)}, bf16[1024,128]{1,0:T(8,128)(2...) custom-call(bf16[1024,1024]{1,0:T(8,128)(2,1)} %bitcast.52, ...), custom_call_target="tpu_custom_call" | custom-call | tf_op jit(solution)/shard_map/attention_forward/pallas_call | solution.py:501
  101.5 1.6 copy-done.1
  103.1 15.8 %scatter_pair.2 = f32[256,1024]{1,0:T(8,128)S(1)} custom-call(bf16[4,256,1024]{2,1,0:T(8,128)(2,1)S(1)} %bitcast.40), custom_call_target="tpu_custom_call" | custom-call | tf_op jit(solution)/shard_map/scatter_pair/pallas_call | solution.py:409
  119.6 1.4 select_reduce_fusion
  121.5 0.7 pad.9.refs_1_
  122.1 26.9 %gather_ring.1 = (bf16[8,256,1024]{2,1,0:T(8,128)(2,1)}, f32[8,256,128]{2,1,0:T(8,128)}) custom-call(bf16[256,1024]{1,0:T(8,128)(2,1)} %copy-done.8, f32[256,128]{1,0:T(8,128)} %pad.9.refs_1_), custom_call_target="tpu_custom_call" | custom-call | tf_op jit(solution)/shard_map/gather_ring/pallas_call | solution.py:167
  149.1 98.5 %experts.1 = (bf16[2048,1024]{1,0:T(8,128)(2,1)}, bf16[2048,1024]{1,0:T(8,128)(2,1)}, f32[2048,128]{1,0:T(8,128)}, bf16[1024,6144]{1,0:T(8,128)(2,1)}) custom-call(bf16[2048,1024]{1,0:T(8,128)(2,1)} %bitcast.50, bf16[2048,1024]{1,0:T(8,128)(2,1)} %bitcast.49, f32[2048,128]{1,0:T(8,128)} %bitcast.53, bf16[1024,6144]{1,0:T(8,128)(2,1)} %all-gather.2.cloned.1.call-done.weights), custom_call_target="tpu_custom_call" | custom-call | tf_op jit(solution)/shard_map/experts/pallas_call | solution.py:696
  247.6 1.3 convert_element_type.86
  248.9 2.7 pad_maximum_fusion
  251.6 27.6 %scatter_ring.1 = f32[256,1152]{1,0:T(8,128)S(1)} custom-call(bf16[8,256,1152]{2,1,0:T(8,128)(2,1)S(1)} %bitcast.38), custom_call_target="tpu_custom_call" | custom-call | tf_op jit(solution)/shard_map/scatter_ring/pallas_call | solution.py:361
  279.4 1.5 multiply_reduce_fusion
  280.9 0.9 copy-done.4
  281.9 1.1 fusion.14.own
  283.0 18.0 %gather_pair.1 = bf16[4,256,1024]{2,1,0:T(8,128)(2,1)} custom-call(bf16[256,1024]{1,0:T(8,128)(2,1)} %fusion.14.own), custom_call_target="tpu_custom_call" | custom-call | tf_op jit(solution)/shard_map/gather_pair/pallas_call | solution.py:225
  301.0 20.4 %attention_backward.1 = (bf16[1024,1024]{1,0:T(8,128)(2,1)}, bf16[1024,768]{1,0:T(8,128)(2,1)}) custom-call(bf16[1024,1024]{1,0:T(8,128)(2,1)} %bitcast.46, bf16[1024,1024]{1,0:T(8,128)(2,1)} %get-tuple-element.41.normed, bf16[1024,896]{1,0:T(8,128)(2,1)} %bitcast.45, f32[1024,128]{1,0:T(8,128)} %constant.25.clone.cosine, f32[1024,128]{1,0:T(8,128)} %constant.26.clone.sine, ...), custom_call_target="tpu_custom_call" | custom-call | tf_op jit(solution)/shard_map/attention_backward/pallas_call | solution.py:574
  322.2 0.9 maximum_maximum_fusion
  323.2 0.5 reduce-scatter.8.cloned.1.call-update
  323.7 72.8 %reduce-scatter.4.cloned.1.call-done = bf16[64,768]{1,0:T(8,128)(2,1)} async-done(((bf16[1024,768]{1,0:T(8,128)(2,1)}), bf16[64,768]{1,0:T(8,128)(2,1)}) %reduce-scatter.4.cloned.1.call-update) | async-done | bytes 98320 | tf_op jit(solution)/shard_map/reduce_scatter | solution.py:830
  396.5 4.3 all-to-all-start.2
  400.8 70.9 %reduce-scatter.6.cloned.1.call-done = bf16[64,128]{1,0:T(8,128)(2,1)} async-done(((bf16[1024,128]{1,0:T(8,128)(2,1)}), bf16[64,128]{1,0:T(8,128)(2,1)}) %reduce-scatter.6.cloned.1.call-update) | async-done | bytes 16400 | tf_op jit(solution)/shard_map/reduce_scatter | solution.py:822
  471.6 1.4 broadcast_in_dim.58
  473.0 4.3 all-to-all-start.4
  477.4 5.5 all-to-all-done.4
  482.9 6.1 %all_to_all.31 = f32[4,1,32]{2,1,0:T(1,128)S(1)} all-to-all(f32[4,1,32]{2,1,0:T(1,128)S(1)} %broadcast_in_dim.54), channel_id=1, replica_groups=mesh['x'=4,'z'=4,'yh'=2,'yl'=2,'core'=2] {'yl','core'}, dimensions={0} | all-to-all | bytes 1024 | tf_op jit(solution)/shard_map/all_to_all | solution.py:726
  489.0 4.7 all-to-all-start.1
  493.8 59.4 %scatter_pair.3 = f32[256,1024]{1,0:T(8,128)S(1)} custom-call(bf16[4,256,1024]{2,1,0:T(8,128)(2,1)S(1)} %bitcast.39), custom_call_target="tpu_custom_call" | custom-call | tf_op jit(solution)/shard_map/scatter_pair/pallas_call | solution.py:409
  553.6 0.7 slice_reduce_fusion
  554.3 0.6 fusion.17
  554.9 0.6 fusion.16
  555.5 0.5 convert_divide_fusion
  556.1 4.3 convert_reduce_fusion
  560.4 8.7 %reduce-scatter.8.cloned.1.call-done = bf16[64,6144]{1,0:T(8,128)(2,1)} async-done(((bf16[1024,6144]{1,0:T(8,128)(2,1)}), bf16[64,6144]{1,0:T(8,128)(2,1)}) %reduce-scatter.8.cloned.1.call-update) | async-done | bytes 786448 | tf_op jit(solution)/shard_map/reduce_scatter | solution.py:805
  569.1 4.3 all-to-all-start.5
  573.4 3.2 fusion.5
  576.6 9.2 %all-to-all-done.5 = bf16[2,32,6144]{2,1,0:T(8,128)(2,1)} async-done(((bf16[2,32,6144]{2,1,0:T(8,128)(2,1)}), bf16[2,32,6144]{2,1,0:T(8,128)(2,1)}, u32[]{:S(2)}, u32[]{:S(2)}) %all-to-all-start.5) | async-done | bytes 786464 | tf_op jit(solution)/shard_map/all_to_all | solution.py:835
  585.8 2.3 reshape.164
  588.1 0.5 copy.69
  588.6 1.2 fusion.15
  (81 shorter events, 3.0 us)
Async XLA Ops:
  7.2 141.9 %all-gather.2.cloned.1.call-start = ((), (), s32[]{:S(2)}) async-start(), calls=%async_computation.9 | async-start | bytes 13369344 | tf_op jit(solution)/shard_map/all_gather | solution.py:769
  8.8 17.5 %copy-start.22 = (bf16[32]{0:T(256)(128)(2,1)S(1)}, bf16[32]{0:T(256)(128)(2,1)}, u32[]{:S(2)}) copy-start(bf16[32]{0:T(256)(128)(2,1)} %param.18) | copy-start | bytes 196
  8.8 17.6 %copy-start.21 = (bf16[32]{0:T(256)(128)(2,1)S(1)}, bf16[32]{0:T(256)(128)(2,1)}, u32[]{:S(2)}) copy-start(bf16[32]{0:T(256)(128)(2,1)} %param.23) | copy-start | bytes 196
  8.9 17.7 %copy-start.20 = (s32[256]{0:T(256)S(1)}, s32[256]{0:T(256)}, u32[]{:S(2)}) copy-start(s32[256]{0:T(256)} %param.29) | copy-start | bytes 3076
  8.9 18.3 %copy-start.12 = (bf16[32,256]{1,0:T(8,128)(2,1)S(1)}, bf16[32,256]{1,0:T(8,128)(2,1)}, u32[]{:S(2)}) copy-start(bf16[32,256]{1,0:T(8,128)(2,1)} %param.19) | copy-start | bytes 49156
  8.9 18.3 %copy-start.15 = (bf16[32,128]{1,0:T(8,128)(2,1)S(1)}, bf16[32,128]{1,0:T(8,128)(2,1)}, u32[]{:S(2)}) copy-start(bf16[32,128]{1,0:T(8,128)(2,1)} %param.20) | copy-start | bytes 24580
  8.9 18.3 %copy-start.16 = (bf16[32,128]{1,0:T(8,128)(2,1)S(1)}, bf16[32,128]{1,0:T(8,128)(2,1)}, u32[]{:S(2)}) copy-start(bf16[32,128]{1,0:T(8,128)(2,1)} %param.21) | copy-start | bytes 24580
  8.9 18.3 %copy-start.17 = (bf16[32,256]{1,0:T(8,128)(2,1)S(1)}, bf16[32,256]{1,0:T(8,128)(2,1)}, u32[]{:S(2)}) copy-start(bf16[32,256]{1,0:T(8,128)(2,1)} %param.22) | copy-start | bytes 49156
  8.9 18.3 %copy-start.18 = (bf16[32,32]{1,0:T(8,128)(2,1)S(1)}, bf16[32,32]{1,0:T(8,128)(2,1)}, u32[]{:S(2)}) copy-start(bf16[32,32]{1,0:T(8,128)(2,1)} %param.24) | copy-start | bytes 6148
  26.3 370.2 %reduce-scatter.4.cloned.1.call-start = ((), (), s32[]{:S(2)}) async-start(), calls=%async_computation.10 | async-start | bytes 1671168 | tf_op jit(solution)/shard_map/reduce_scatter | solution.py:830
  69.9 3.0 copy-start.14
  73.0 45.9 %copy-start.19 = (s32[256,8]{0,1:T(8,128)S(1)}, s32[256,8]{0,1:T(8,128)}, u32[]{:S(2)}) copy-start(s32[256,8]{0,1:T(8,128)} %param.28) | copy-start | bytes 24580
  73.0 46.1 %copy-start.6 = (bf16[256,1024]{1,0:T(8,128)(2,1)S(1)}, bf16[256,1024]{1,0:T(8,128)(2,1)}, u32[]{:S(2)}) copy-start(bf16[256,1024]{1,0:T(8,128)(2,1)} %hidden.1) | copy-start | bytes 1572868
  101.5 1.6 copy-start.1
  119.4 161.5 %copy-start.2 = (f32[256,1024]{1,0:T(8,128)}, f32[256,1024]{1,0:T(8,128)S(1)}, u32[]{:S(2)}) copy-start(f32[256,1024]{1,0:T(8,128)S(1)} %get-tuple-element.55) | copy-start | bytes 3145732
  119.6 2.6 copy-start.8
  279.2 2.7 copy-start.10
  280.9 1.0 copy-start.4
  301.0 20.6 %copy-start.9 = (bf16[256,1024]{1,0:T(8,128)(2,1)S(1)}, bf16[256,1024]{1,0:T(8,128)(2,1)}, u32[]{:S(2)}) copy-start(bf16[256,1024]{1,0:T(8,128)(2,1)} %copy-done.8) | copy-start | bytes 1572868
  321.5 150.1 %reduce-scatter.6.cloned.1.call-start = ((), (), s32[]{:S(2)}) async-start(), calls=%async_computation.11 | async-start | bytes 278528 | tf_op jit(solution)/shard_map/reduce_scatter | solution.py:822
  323.1 245.9 %reduce-scatter.8.cloned.1.call-start = ((), (), s32[]{:S(2)}) async-start(), calls=%async_computation.12 | async-start | bytes 13369344 | tf_op jit(solution)/shard_map/reduce_scatter | solution.py:805
  396.5 75.2 %all-to-all-start.2 = ((bf16[2,32,768]{2,1,0:T(8,128)(2,1)}), bf16[2,32,768]{2,1,0:T(8,128)(2,1)S(1)}, u32[]{:S(2)}, u32[]{:S(2)}) async-start(bf16[2,32,768]{2,1,0:T(8,128)(2,1)} %bitcast.61), calls=%async_computation.3 | async-start | bytes 196608 | tf_op jit(solution)/shard_map/all_to_all | solution.py:837
  473.0 9.9 %all-to-all-start.4 = ((bf16[8,32,128]{2,1,0:T(8,128)(2,1)}), bf16[8,32,128]{2,1,0:T(8,128)(2,1)S(1)}, u32[]{:S(2)}, u32[]{:S(2)}) async-start(bf16[8,32,128]{2,1,0:T(8,128)(2,1)} %bitcast.23), calls=%async_computation.6 | async-start | bytes 131072 | tf_op jit(solution)/shard_map/all_to_all | solution.py:825
  489.0 4.8 copy-start
  489.0 67.1 %all-to-all-start.1 = ((bf16[8,256,1024]{2,1,0:T(8,128)(2,1)}), bf16[8,256,1024]{2,1,0:T(8,128)(2,1)}, u32[]{:S(2)}, u32[]{:S(2)}) async-start(bf16[8,256,1024]{2,1,0:T(8,128)(2,1)} %bitcast.48), calls=%async_computation.1 | async-start | bytes 8388608 | tf_op jit(solution)/shard_map/all_to_all | solution.py:732
  493.7 59.5 %copy-start.7 = (bf16[256,1024]{1,0:T(8,128)(2,1)S(1)}, bf16[256,1024]{1,0:T(8,128)(2,1)}, u32[]{:S(2)}) copy-start(bf16[256,1024]{1,0:T(8,128)(2,1)} %hidden.1) | copy-start | bytes 1572868
  493.7 59.5 %copy-start.13 = (f32[1024]{0:T(1024)S(1)}, f32[1024]{0:T(1024)}, u32[]{:S(2)}) copy-start(f32[1024]{0:T(1024)} %get-tuple-element.53) | copy-start | bytes 12292
  553.6 6.8 %copy-start.11 = (f32[32,128]{1,0:T(8,128)}, f32[32,128]{1,0:T(8,128)S(1)}, u32[]{:S(2)}) copy-start(f32[32,128]{1,0:T(8,128)S(1)} %convert_reduce_fusion.4) | copy-start | bytes 49156
  556.1 17.3 %copy-start.5 = (f32[256,1024]{1,0:T(8,128)S(1)}, f32[256,1024]{1,0:T(8,128)}, u32[]{:S(2)}) copy-start(f32[256,1024]{1,0:T(8,128)} %copy-done.4) | copy-start | bytes 3145732
  560.4 13.0 %copy-start.3 = (f32[256,1024]{1,0:T(8,128)S(1)}, f32[256,1024]{1,0:T(8,128)}, u32[]{:S(2)}) copy-start(f32[256,1024]{1,0:T(8,128)} %copy-done.2) | copy-start | bytes 3145732
  569.1 16.7 %all-to-all-start.5 = ((bf16[2,32,6144]{2,1,0:T(8,128)(2,1)}), bf16[2,32,6144]{2,1,0:T(8,128)(2,1)}, u32[]{:S(2)}, u32[]{:S(2)}) async-start(bf16[2,32,6144]{2,1,0:T(8,128)(2,1)} %bitcast.54), calls=%async_computation.8 | async-start | bytes 1572864 | tf_op jit(solution)/shard_map/all_to_all | solution.py:835
Sparse Core Ops, SparseCore 0:
  26.4 96.8 all-gather.1
  321.6 74.8 reduce-scatter.3
  400.2 71.3 reduce-scatter.5
  475.3 93.7 reduce-scatter.7
